TPU v7x, 32 devices: a whole 2x2x4 slice. The times are simulated.
32 devices in a mesh: user: 8 (over z, core), item: 4 (over y, x).
Axes of the slice: x: 2, y: 2, z: 4, core: 2. Of those that a mesh axis runs over, the one named last changes fastest.
Arguments:
- user_factors: float32 [4096, 256], P('user'), may hold values from -0.3 to 0.3, as said below
- item_factors: float32 [2048, 256], P('item'), may hold values from -0.6 to 0.6
- tile_user: int32 [4, 8, 8, 2], P('item', 'user'), may hold values from 0 to 3
- tile_item: int32 [4, 8, 8, 2], P('item', 'user'), may hold values from 0 to 3
- tile_count: int32 [4, 8, 8], P('item', 'user'), may hold values from 1 to 2, as said below
- tile_conf: bfloat16 [4, 8, 8, 2, 128, 128], P('item', 'user'), may hold values from 0.099609375 to 4
- held_user: int32 [8, 4, 4, 2], P('user', 'item'), may hold values from 0 to 1
- held_item: int32 [8, 4, 4, 2], P('user', 'item'), may hold values from 0 to 3
- held_count: int32 [8, 4, 4], P('user', 'item'), may hold values from 1 to 2, as said below
- held_conf: bfloat16 [8, 4, 4, 2, 128, 128], P('user', 'item'), may hold values from 0.099609375 to 4
Outputs:
- new_items: float32 [2048, 256], P('item')
- folded_users: float32 [2048, 256], P('user')
Inputs may be any that keep to these rules, and one draw needn't show every extreme that they name: `user_factors`: user factors; the scale of a factor column varies by up to a factor of ten. `tile_count`: some device has an owner with all 2 slots live and one with a single live slot. `held_count`: some device has an owner with all 2 slots live and one with a single live slot.
All inputs are finite; a program needn't handle non-finite values.
Results may differ from a plain program's by a relative error of at most 0.0003.
Values may be sent and summed in bfloat16 or wider, within the bound.
A program may use at most 128 MiB of HBM per device.

v0:
```python
import jax
import jax.numpy as jnp
from jax import lax
from jax.sharding import PartitionSpec as P

HB_DEV = 2
ITERS = 2


highest = lax.Precision.HIGHEST
ridge_weight = 1.0
epsilon = 1e-06


def local_gram(rows):
    return jnp.einsum("nk,nm->km", rows, rows, precision=highest)


def gram_apply(vector, gram):
    return jnp.einsum("jck,km->jcm", vector, gram, precision=highest) + ridge_weight * vector


def block_onehot(positions, blocks):
    return (positions[:, None] == jnp.arange(blocks, dtype=jnp.int32)[None, :]).astype(jnp.float32)


def item_terms(factors, weights, positions, onehot, vector):
    picked = vector[positions]
    scores = jnp.einsum("tuk,tik->tui", factors, picked, precision=highest) * weights
    terms = jnp.einsum("tui,tuk->tik", scores, factors, precision=highest)
    return jnp.einsum("tj,tik->jik", onehot, terms, precision=highest)


def item_right(factors, right_weights, onehot):
    terms = jnp.einsum("tui,tuk->tik", right_weights, factors, precision=highest)
    return jnp.einsum("tj,tik->jik", onehot, terms, precision=highest)


def held_terms(factors, weights, positions, onehot, vector):
    picked = vector[positions]
    scores = jnp.einsum("tik,thk->thi", factors, picked, precision=highest) * weights
    terms = jnp.einsum("thi,tik->thk", scores, factors, precision=highest)
    return jnp.einsum("tj,thk->jhk", onehot, terms, precision=highest)


def held_right(factors, right_weights, onehot):
    terms = jnp.einsum("thi,tik->thk", right_weights, factors, precision=highest)
    return jnp.einsum("tj,thk->jhk", onehot, terms, precision=highest)


def conjugate(operator, residual, start):
    solution = start
    direction = residual
    norm_now = jnp.sum(residual * residual, axis=-1, keepdims=True)
    for iteration in range(ITERS):
        image = operator(direction)
        alpha = norm_now / (jnp.sum(direction * image, axis=-1, keepdims=True) + epsilon)
        solution = solution + alpha * direction
        residual = residual - alpha * image
        norm_next = jnp.sum(residual * residual, axis=-1, keepdims=True)
        direction = residual + norm_next / (norm_now + epsilon) * direction
        norm_now = norm_next
    return solution


def user_total(partial_value):
    return lax.psum(partial_value, "user")


def item_total(partial_value):
    return lax.psum(partial_value, "item")


def tile_weights(confidence, live_slots, tile_width):
    live_flat = live_slots.reshape(-1).astype(jnp.float32)[:, None, None]
    conf_flat = confidence.reshape(-1, tile_width, tile_width).astype(jnp.float32)
    return (conf_flat * live_flat, (1.0 + conf_flat) * live_flat)


def shards(
    user_factors,
    item_factors,
    tile_user,
    tile_item,
    tile_count,
    tile_conf,
    held_user,
    held_item,
    held_count,
    held_conf,
):
    factor_rank = user_factors.shape[1]
    tile_width = tile_conf.shape[-1]
    user_peers = lax.axis_size("user")
    item_peers = lax.axis_size("item")
    user_index = tile_user[0, 0]
    item_index = tile_item[0, 0]
    slot_count = user_index.shape[1]
    live_slots = (
        jnp.arange(slot_count, dtype=jnp.int32)[None, :] < tile_count[0, 0][:, None]
    ).astype(jnp.int32)
    confidence = tile_conf[0, 0]
    whole_users = lax.all_gather(user_factors, "user", axis=0, tiled=True)
    gram_users = lax.psum(local_gram(user_factors), "user")
    user_table = whole_users.reshape(user_peers, -1, tile_width, factor_rank)
    tile_factors = user_table[jnp.arange(user_peers, dtype=jnp.int32)[:, None], user_index]
    factors = tile_factors.reshape(-1, tile_width, factor_rank)
    weights, right_weights = tile_weights(confidence, live_slots, tile_width)
    item_blocks = item_factors.shape[0] // tile_width
    positions = item_index.reshape(-1)
    onehot = block_onehot(positions, item_blocks)
    warm_start = item_factors.reshape(item_blocks, tile_width, factor_rank)

    def item_operator(direction):
        return user_total(item_terms(factors, weights, positions, onehot, direction)) + gram_apply(
            direction, gram_users
        )

    start_total = user_total(
        item_right(factors, right_weights, onehot)
        - item_terms(factors, weights, positions, onehot, warm_start)
    )
    residual = start_total - gram_apply(warm_start, gram_users)
    own_items = conjugate(item_operator, residual, warm_start)
    new_items = own_items.reshape(-1, factor_rank)
    held_index = held_user[0, 0]
    owner_index = held_item[0, 0]
    held_slots = owner_index.shape[1]
    held_live = (
        jnp.arange(held_slots, dtype=jnp.int32)[None, :] < held_count[0, 0][:, None]
    ).astype(jnp.int32)
    held_confidence = held_conf[0, 0]
    whole_items = lax.all_gather(new_items, "item", axis=0, tiled=True)
    gram_items = lax.psum(local_gram(new_items), "item")
    item_table = whole_items.reshape(item_peers, -1, tile_width, factor_rank)
    held_factors = item_table[jnp.arange(item_peers, dtype=jnp.int32)[:, None], owner_index]
    held_flat = held_factors.reshape(-1, tile_width, factor_rank)
    held_weights, held_right_weights = tile_weights(held_confidence, held_live, tile_width)
    held_positions = held_index.reshape(-1)
    held_onehot = block_onehot(held_positions, HB_DEV)

    def held_operator(direction):
        return item_total(
            held_terms(held_flat, held_weights, held_positions, held_onehot, direction)
        ) + gram_apply(direction, gram_items)

    held_residual = item_total(held_right(held_flat, held_right_weights, held_onehot))
    zero_start = jnp.zeros((HB_DEV, tile_width, factor_rank), jnp.float32)
    folded_users = conjugate(held_operator, held_residual, zero_start).reshape(-1, factor_rank)
    return (new_items, folded_users)


def solution(mesh):
    in_specs = (
        P("user", None),
        P("item", None),
        P("item", "user", None, None),
        P("item", "user", None, None),
        P("item", "user", None),
        P("item", "user", None, None, None, None),
        P("user", "item", None, None),
        P("user", "item", None, None),
        P("user", "item", None),
        P("user", "item", None, None, None, None),
    )
    out_specs = (P("item", None), P("user", None))
    return jax.shard_map(shards, mesh=mesh, in_specs=in_specs, out_specs=out_specs, check_vma=False)
```

profile of v0, /device:TPU:0, one launch (start us, length us, event | category | flops | bytes accessed | tf_op | source)
XLA Modules:
  0.0 462.1 jit_solution(4443090839881667092)
XLA Ops:
  10.6 3.1 gather_fusion.1
  13.7 1.7 fusion.61
  15.4 44.1 %all-gather.3.cloned.1.call-done = f32[4096,256]{1,0:T(8,128)} async-done(((f32[512,256]{1,0:T(8,128)}), f32[4096,256]{1,0:T(8,128)}) %all-gather.3.cloned.1.call-update) | async-done | bytes 4194320 | tf_op jit(solution)/shard_map/all_gather | solution.py:103
  59.5 2.9 gather_fusion
  62.4 2.1 fusion.19
  64.5 2.1 convolution_multiply_fusion.2
  66.6 2.0 fusion.60
  68.7 2.0 fusion.4
  70.6 2.0 fusion.6
  73.8 56.2 %all-reduce.17.cloned.1.call-done = (f32[4,128,256]{2,1,0:T(8,128)}, f32[256,256]{1,0:T(8,128)}) async-done(((f32[4,128,256]{2,1,0:T(8,128)}, f32[256,256]{1,0:T(8,128)}), (f32[4,128,256]{2,1,0:T(8,128)}, f32[256,256]{1,0:T(8,128)})) %all-reduce.17.cloned.1.call-update) | async-done | bytes 786448 | tf_op jit(solution)/shard_map/psum | solution.py:67
  130.0 1.7 fusion.9
  131.8 2.0 gather_fusion.2
  133.8 3.7 convolution_multiply_fusion.1
  137.5 2.0 fusion.62
  139.5 2.0 fusion.2
  142.7 55.1 %all-reduce.9.cloned.1.call-done = f32[4,128,256]{2,1,0:T(8,128)} async-done(((f32[4,128,256]{2,1,0:T(8,128)}), f32[4,128,256]{2,1,0:T(8,128)}) %all-reduce.9.cloned.1.call-update) | async-done | bytes 524304 | tf_op jit(solution)/shard_map/psum | solution.py:67
  197.8 1.7 multiply_reduce_fusion.1
  200.1 2.0 gather_fusion.3
  202.1 3.8 convolution_multiply_fusion
  205.8 2.0 fusion.63
  207.9 2.0 fusion
  210.9 55.2 %all-reduce.11.cloned.1.call-done = f32[4,128,256]{2,1,0:T(8,128)} async-done(((f32[4,128,256]{2,1,0:T(8,128)}), f32[4,128,256]{2,1,0:T(8,128)}) %all-reduce.11.cloned.1.call-update) | async-done | bytes 524304 | tf_op jit(solution)/shard_map/psum | solution.py:67
  266.1 1.7 fusion.13
  269.5 33.8 %all-gather.5.cloned.1.call-done = f32[2048,256]{1,0:T(8,128)} async-done(((f32[512,256]{1,0:T(8,128)}), f32[2048,256]{1,0:T(8,128)}) %all-gather.5.cloned.1.call-update) | async-done | bytes 2097168 | tf_op jit(solution)/shard_map/all_gather | solution.py:133
  303.3 2.2 gather_fusion.4
  308.8 1.7 convolution_bitcast_fusion.1
  310.5 41.0 %all-reduce.13.cloned.1.call-done = f32[2,128,256]{2,1,0:T(8,128)} async-done(((f32[2,128,256]{2,1,0:T(8,128)}), f32[2,128,256]{2,1,0:T(8,128)}) %all-reduce.13.cloned.1.call-update) | async-done | bytes 262160 | tf_op jit(solution)/shard_map/psum | solution.py:71
  351.6 1.6 gather_fusion.5
  357.3 45.6 %all-reduce.19.cloned.1.call-done = (f32[2,128,256]{2,1,0:T(8,128)}, f32[256,256]{1,0:T(8,128)}) async-done(((f32[2,128,256]{2,1,0:T(8,128)}, f32[256,256]{1,0:T(8,128)}), (f32[2,128,256]{2,1,0:T(8,128)}, f32[256,256]{1,0:T(8,128)})) %all-reduce.19.cloned.1.call-update) | async-done | bytes 524304 | tf_op jit(solution)/shard_map/psum | solution.py:71
  402.8 1.5 multiply_reduce_fusion.4
  409.4 43.1 %all-reduce.15.cloned.1.call-done = f32[2,128,256]{2,1,0:T(8,128)} async-done(((f32[2,128,256]{2,1,0:T(8,128)}), f32[2,128,256]{2,1,0:T(8,128)}) %all-reduce.15.cloned.1.call-update) | async-done | bytes 262160 | tf_op jit(solution)/shard_map/psum | solution.py:71
  452.5 1.4 fusion.17
  (91 shorter events, 22.1 us)
Async XLA Ops:
  7.2 52.3 %all-gather.3.cloned.1.call-start = ((), (), s32[]{:S(2)}) async-start(), calls=%async_computation | async-start | bytes 4718592 | tf_op jit(solution)/shard_map/all_gather | solution.py:103
  7.9 122.1 %all-reduce.17.cloned.1.call-start = ((), (), s32[]{:S(2)}) async-start(), calls=%async_computation.6 | async-start | bytes 1572864 | tf_op jit(solution)/shard_map/psum | solution.py:67
  10.5 3.1 copy-start.7
  59.5 2.9 copy-start.3
  62.4 2.1 copy-start.5
  70.6 59.4 %copy-start = (f32[512,256]{1,0:T(8,128)S(1)}, f32[512,256]{1,0:T(8,128)}, u32[]{:S(2)}) copy-start(f32[512,256]{1,0:T(8,128)} %param.11) | copy-start | bytes 1572868
  73.6 124.2 %all-reduce.9.cloned.1.call-start = ((), (), s32[]{:S(2)}) async-start(), calls=%async_computation.1 | async-start | bytes 1048576 | tf_op jit(solution)/shard_map/psum | solution.py:67
  131.8 2.0 copy-start.4
  139.5 58.3 %copy-start.9 = (f32[256,256]{1,0:T(8,128)S(1)}, f32[256,256]{1,0:T(8,128)}, u32[]{:S(2)}) copy-start(f32[256,256]{1,0:T(8,128)} %get-tuple-element.7) | copy-start | bytes 786436
  142.4 123.6 %all-reduce.11.cloned.1.call-start = ((), (), s32[]{:S(2)}) async-start(), calls=%async_computation.2 | async-start | bytes 1048576 | tf_op jit(solution)/shard_map/psum | solution.py:67
  209.9 57.9 %copy-start.1 = (f32[512,256]{1,0:T(8,128)S(1)}, f32[512,256]{1,0:T(8,128)}, u32[]{:S(2)}) copy-start(f32[512,256]{1,0:T(8,128)} %param.11) | copy-start | bytes 1572868
  210.8 58.1 %copy-start.11 = (s32[1,1,4,2]{2,3,1,0:T(2,128)S(1)}, s32[1,1,4,2]{2,3,1,0:T(2,128)}, u32[]{:S(2)}) copy-start(s32[1,1,4,2]{2,3,1,0:T(2,128)} %param.16) | copy-start | bytes 100
  210.8 58.3 %copy-start.12 = (s32[1,1,4,2]{2,3,1,0:T(2,128)S(1)}, s32[1,1,4,2]{2,3,1,0:T(2,128)}, u32[]{:S(2)}) copy-start(s32[1,1,4,2]{2,3,1,0:T(2,128)} %param.17) | copy-start | bytes 100
  210.8 58.5 %copy-start.13 = (s32[1,1,4]{2,1,0:T(1,128)S(1)}, s32[1,1,4]{2,1,0:T(1,128)}, u32[]{:S(2)}) copy-start(s32[1,1,4]{2,1,0:T(1,128)} %param.18) | copy-start | bytes 52
  210.8 92.4 %all-gather.5.cloned.1.call-start = ((), (), s32[]{:S(2)}) async-start(), calls=%async_computation.3 | async-start | bytes 2621440 | tf_op jit(solution)/shard_map/all_gather | solution.py:133
  267.8 37.7 %copy-start.8 = (bf16[1,1,4,2,128,128]{5,4,3,2,1,0:T(8,128)(2,1)S(1)}, bf16[1,1,4,2,128,128]{5,4,3,2,1,0:T(8,128)(2,1)}, u32[]{:S(2)}) copy-start(bf16[1,1,4,2,128,128]{5,4,3,2,1,0:T(8,128)(2,1)} %param.19) | copy-start | bytes 786436
  268.8 82.8 %all-reduce.13.cloned.1.call-start = ((), (), s32[]{:S(2)}) async-start(), calls=%async_computation.4 | async-start | bytes 524288 | tf_op jit(solution)/shard_map/psum | solution.py:71
  305.5 3.3 copy-start.6
  308.5 94.3 %all-reduce.19.cloned.1.call-start = ((), (), s32[]{:S(2)}) async-start(), calls=%async_computation.7 | async-start | bytes 1048576 | tf_op jit(solution)/shard_map/psum | solution.py:71
  354.3 48.6 %copy-start.2 = (f32[2,128,256]{2,1,0:T(8,128)S(1)}, f32[2,128,256]{2,1,0:T(8,128)}, u32[]{:S(2)}) copy-start(f32[2,128,256]{2,1,0:T(8,128)} %all-reduce.13.cloned.1.call-done) | copy-start | bytes 786436
  357.2 95.3 %all-reduce.15.cloned.1.call-start = ((), (), s32[]{:S(2)}) async-start(), calls=%async_computation.5 | async-start | bytes 524288 | tf_op jit(solution)/shard_map/psum | solution.py:71
  406.5 46.0 %copy-start.10 = (f32[256,256]{1,0:T(8,128)S(1)}, f32[256,256]{1,0:T(8,128)}, u32[]{:S(2)}) copy-start(f32[256,256]{1,0:T(8,128)} %get-tuple-element.9) | copy-start | bytes 786436
Sparse Core Ops, SparseCore 0:
  9.6 49.8 all-gather.2
  73.7 56.2 all-reduce.16
  142.5 55.2 all-reduce.8
  210.9 55.0 all-reduce.10
  268.9 34.2 all-gather.4
  308.6 42.9 all-reduce.12
  357.3 45.4 all-reduce.18
  409.6 42.9 all-reduce.14
where the time goes:
time: 471 us; the launch traced here: 462 us
  waiting for transfers between devices  375 us (80%)
  matrix products  46 us (10%)
  local copies, waits for them, and re-layouts  20.1 us (4%)
  between operations  15 us (3%)
  other arithmetic  5.18 us (1%)
    psum x3, waiting for transfers between devices, user_total(): return lax.psum(partial_value, 'user')  167 us
    psum x3, waiting for transfers between devices, item_total(): return lax.psum(partial_value, 'item')  130 us
    all_gather x1, waiting for transfers between devices, shards(): whole_users = lax.all_gather(user_factors, 'user', axis=0, tiled=True)  44.1 us
    all_gather x1, waiting for transfers between devices, shards(): whole_items = lax.all_gather(new_items, 'item', axis=0, tiled=True)  33.8 us
    dot_general x3, matrix products, item_terms(): jnp.einsum('tuk,tik->tui', factors, picked, precision=highest) * weights  9.55 us
  transfers between devices with their start and end apart: 8, of which 8 were waited for; matrix products, arithmetic and copies ran while one was open for 2% of the time, Pallas kernels for 0%

commit v1 on v0

v1 whole, which is shorter than its diff:
```python
import functools

import jax
import jax.numpy as jnp
from jax import lax
from jax.experimental import pallas as pl
from jax.experimental.pallas import tpu as pltpu
from jax.sharding import PartitionSpec as P

ITERS = 2
RIDGE = 1.0
EPS = 1e-6
MESH = pl.DeviceIdType.MESH
ANY = pl.BlockSpec(memory_space=pl.ANY)
VMEM = pl.BlockSpec(memory_space=pltpu.VMEM)
SMEM = pl.BlockSpec(memory_space=pltpu.SMEM)


def place(users, items):
    u = lax.axis_index("user")
    return lax.axis_index("item"), u, u // 2, lax.rem(u, 2)


def greet(devices):
    barrier = pltpu.get_barrier_semaphore()
    for device in devices:
        pl.semaphore_signal(barrier, inc=1, device_id=device, device_id_type=MESH)
    pl.semaphore_wait(barrier, len(devices))


def send(src, dst, send_sem, recv_sem, device):
    copy = pltpu.make_async_remote_copy(
        src_ref=src, dst_ref=dst, send_sem=send_sem, recv_sem=recv_sem, device_id=device, device_id_type=MESH
    )
    copy.start()
    return copy


def pack_rows(tile_of, out, slots, peers):
    rows = out.shape[1] // slots
    group = max(1, 16 // rows)
    for first in range(0, slots, group):
        tiles = [tile_of(first + k) for k in range(group)]
        for p in range(peers):
            part = [t[p * rows:(p + 1) * rows] for t in tiles]
            part = part[0] if group == 1 else jnp.concatenate(part, axis=0)
            out[p, first * rows:(first + group) * rows, :] = part.astype(out.dtype)


def spread_kernel(users, items, y_ref, conf_ref, held_ref, meta_ref,
                  y_out, c_out, h_out, mu_out, mi_out, c_send, h_send,
                  z_s, z_r, xy_s, xy_r, sib_s, sib_r, own_s, own_r,
                  c_s, c_r, h_s, h_r, mu_s, mu_r, mi_s, mi_r, local):
    zs = users // 2
    i, u, z, c = place(users, items)
    sibling = (2 * z + 1 - c, i)
    quarter = y_ref.shape[1]
    user_peers = [lax.rem(u + k, users) for k in range(1, users)]
    item_peers = [lax.rem(i + e, items) for e in range(1, items)]
    greet([(p, i) for p in user_peers] + [(u, p) for p in item_peers])

    pending = []
    crossing = []
    for d in range(1, zs):
        peer = 2 * lax.rem(z + d, zs) + c
        crossing.append(send(y_ref.at[i], y_out.at[u, i], z_s.at[d], z_r.at[d], (peer, i)))
    pending.append(send(y_ref, y_out.at[u], own_s, own_r, sibling))
    keep = [pltpu.make_async_copy(y_ref, y_out.at[u], local.at[0])]
    keep[0].start()
    for k, p in enumerate(user_peers):
        pending.append(send(meta_ref, mu_out.at[u], mu_s.at[k], mu_r.at[k], (p, i)))
    for e, p in enumerate(item_peers):
        pending.append(send(meta_ref, mi_out.at[i], mi_s.at[e], mi_r.at[e], (u, p)))

    slots = conf_ref.shape[0]
    pack_rows(lambda s: conf_ref[s].astype(jnp.float32).T, c_send, slots, users)
    for k, p in enumerate(user_peers):
        pending.append(send(c_send.at[p], c_out.at[u], c_s.at[k], c_r.at[k], (p, i)))
    held_slots = held_ref.shape[0]
    pack_rows(lambda s: held_ref[s].astype(jnp.float32), h_send, held_slots, items)
    for e, p in enumerate(item_peers):
        pending.append(send(h_send.at[p], h_out.at[i], h_s.at[e], h_r.at[e], (u, p)))
    keep.append(pltpu.make_async_copy(c_send.at[u], c_out.at[u], local.at[1]))
    keep.append(pltpu.make_async_copy(h_send.at[i], h_out.at[i], local.at[2]))
    keep.append(pltpu.make_async_copy(meta_ref, mu_out.at[u], local.at[3]))
    keep.append(pltpu.make_async_copy(meta_ref, mi_out.at[i], local.at[4]))
    for copy in keep[1:]:
        copy.start()

    across = {}
    for d in range(1, zs):
        crossing[d - 1].wait_recv()
        shard = 2 * lax.rem(z - d + zs, zs) + c
        block = y_out.at[shard, i]
        for e, p in enumerate(item_peers):
            across[d, e] = send(block, block, xy_s.at[d, e], xy_r.at[d, e], (u, p))
        pending.append(send(block, block, sib_s.at[d, items - 1], sib_r.at[d, items - 1], sibling))
    for d in range(1, zs):
        shard = 2 * lax.rem(z - d + zs, zs) + c
        for e in range(items - 1):
            across[d, e].wait_recv()
            block = y_out.at[shard, lax.rem(i - e - 1 + items, items)]
            pending.append(send(block, block, sib_s.at[d, e], sib_r.at[d, e], sibling))
    for copy in crossing + list(across.values()):
        copy.wait_send()
    for copy in pending:
        copy.wait()
    for copy in keep:
        copy.wait()


def spread(users, items, factors, conf, held, meta):
    rows, rank = factors.shape
    slots, width = conf.shape[0], conf.shape[1]
    held_slots = held.shape[0]
    zs = users // 2
    c_piece = (slots * width // users, width)
    h_piece = (held_slots * width // items, width)
    dma = pltpu.SemaphoreType.DMA
    return pl.pallas_call(
        functools.partial(spread_kernel, users, items),
        out_shape=[
            jax.ShapeDtypeStruct((users, items, rows // items, rank), jnp.float32),
            jax.ShapeDtypeStruct((users,) + c_piece, jnp.bfloat16),
            jax.ShapeDtypeStruct((items,) + h_piece, jnp.bfloat16),
            jax.ShapeDtypeStruct((users,) + meta.shape, jnp.int32),
            jax.ShapeDtypeStruct((items,) + meta.shape, jnp.int32),
        ],
        in_specs=[ANY, VMEM, VMEM, VMEM],
        out_specs=[ANY] * 5,
        scratch_shapes=[
            pltpu.VMEM((users,) + c_piece, jnp.bfloat16),
            pltpu.VMEM((items,) + h_piece, jnp.bfloat16),
            dma((zs,)), dma((zs,)), dma((zs, items)), dma((zs, items)), dma((zs, items)), dma((zs, items)),
            dma, dma, dma((users,)), dma((users,)), dma((items,)), dma((items,)),
            dma((users,)), dma((users,)), dma((items,)), dma((items,)), dma((5,)),
        ],
        compiler_params=pltpu.CompilerParams(
            collective_id=0, has_side_effects=True, vmem_limit_bytes=16 * 2**20
        ),
        name="spread_inputs",
    )(factors.reshape(items, rows // items, rank), conf, held, meta)


def halves(value):
    high = value.astype(jnp.bfloat16)
    return high, (value - high.astype(jnp.float32)).astype(jnp.bfloat16)


def dot(a, b, contract):
    return lax.dot_general(a, b, (((1,), (contract,)), ((), ())), preferred_element_type=jnp.float32)


def product(value, high, low, contract):
    n = value.shape[0]
    top, bottom = halves(value)
    both = dot(jnp.concatenate([top, bottom], axis=0), high, contract)
    return both[:n] + both[n:] + dot(top, low, contract)


def solve_kernel(warm, by_owner, codes_ref, table_ref, tiles_ref, *rest):
    if warm:
        start_ref, out_ref, high, low, weight, right = rest
    else:
        out_ref, high, low, weight, right = rest
    blocks, rows, width = weight.shape
    sources, piece = tiles_ref.shape[0], tiles_ref.shape[1]
    rank = table_ref.shape[1]
    slots = codes_ref.shape[1]
    part = piece // slots
    cap = slots // by_owner
    per_owner = blocks // by_owner
    chunk = 4
    span = chunk * width

    def prepare(b, carry):
        weight[b] = jnp.ones((rows, width), jnp.float32)
        right[b] = jnp.zeros((rows, width), jnp.float32)
        at = pl.ds(pl.multiple_of(b * width, width), width)
        top, bottom = halves(table_ref[at, :])
        high[at, :] = top
        low[at, :] = bottom
        return carry

    lax.fori_loop(0, blocks, prepare, 0)

    def place_tiles(source, carry):
        for s in range(slots):
            code = codes_ref[source, s]

            @pl.when(code >= 0)
            def _():
                block = (s // cap) * per_owner + lax.rem(code, per_owner)
                at = pl.ds(pl.multiple_of((code // per_owner) * part, part), part)
                tile = tiles_ref[source, s * part:(s + 1) * part, :].astype(jnp.float32)
                weight[block, at, :] += tile
                right[block, at, :] += tile + 1.0

        return carry

    lax.fori_loop(0, sources, place_tiles, 0)

    def wide(ref, n):
        return jnp.concatenate([ref[n * chunk + k] for k in range(chunk)], axis=1)

    def sweep(coefficients):
        def step(n, total):
            at = pl.ds(pl.multiple_of(n * span, span), span)
            top, bottom = high[at, :], low[at, :]
            return total + product(coefficients(n, top, bottom), top, bottom, 0)

        return lax.fori_loop(0, blocks // chunk, step, jnp.zeros((rows, rank), jnp.float32), unroll=2)

    def operator(vector):
        return sweep(lambda n, top, bottom: product(vector, top, bottom, 1) * wide(weight, n)) + RIDGE * vector

    if warm:
        x = start_ref[...]
        residual = sweep(
            lambda n, top, bottom: wide(right, n) - product(x, top, bottom, 1) * wide(weight, n)
        ) - RIDGE * x
    else:
        x = jnp.zeros((rows, rank), jnp.float32)
        residual = sweep(lambda n, top, bottom: wide(right, n))
    direction = residual
    norm = jnp.sum(residual * residual, axis=1, keepdims=True)
    for iteration in range(ITERS):
        image = operator(direction)
        alpha = norm / (jnp.sum(direction * image, axis=1, keepdims=True) + EPS)
        x = x + alpha * direction
        if iteration + 1 < ITERS:
            residual = residual - alpha * image
            following = jnp.sum(residual * residual, axis=1, keepdims=True)
            direction = residual + following / (norm + EPS) * direction
            norm = following
    out_ref[...] = x


def solve(codes, table, tiles, rows, by_owner, start=None):
    width = tiles.shape[2]
    count, rank = table.shape
    blocks = count // width
    warm = start is not None
    args = [codes, table, tiles] + ([start] if warm else [])
    return pl.pallas_call(
        functools.partial(solve_kernel, warm, by_owner),
        out_shape=jax.ShapeDtypeStruct((rows, rank), jnp.float32),
        in_specs=[SMEM] + [VMEM] * (len(args) - 1),
        out_specs=VMEM,
        scratch_shapes=[
            pltpu.VMEM((count, rank), jnp.bfloat16),
            pltpu.VMEM((count, rank), jnp.bfloat16),
            pltpu.VMEM((blocks, rows, width), jnp.float32),
            pltpu.VMEM((blocks, rows, width), jnp.float32),
        ],
        compiler_params=pltpu.CompilerParams(vmem_limit_bytes=40 * 2**20),
        name="solve_items" if warm else "solve_held",
    )(*args)


def gather_items_kernel(users, items, x_ref, x_out, z_s, z_r, xy_s, xy_r, sib_s, sib_r, local):
    zs = users // 2
    i, u, z, c = place(users, items)
    sibling = (2 * z + 1 - c, i)
    z_peers = [2 * lax.rem(z + d, zs) + c for d in range(1, zs)]
    item_peers = [lax.rem(i + e, items) for e in range(1, items)]
    greet([(p, i) for p in z_peers] + [(u, p) for p in item_peers] + [sibling])

    crossing, across, pending = [], {}, []
    own = x_out.at[i, :, u]
    for d, p in enumerate(z_peers):
        crossing.append(send(x_ref, own, z_s.at[d], z_r.at[d], (p, i)))
    for e, p in enumerate(item_peers):
        across[0, e] = send(x_ref, own, xy_s.at[0, e], xy_r.at[0, e], (u, p))
    pending.append(send(x_ref, own, sib_s.at[0, items - 1], sib_r.at[0, items - 1], sibling))
    keep = pltpu.make_async_copy(x_ref, own, local)
    keep.start()
    for d in range(1, zs):
        crossing[d - 1].wait_recv()
        block = x_out.at[i, :, 2 * lax.rem(z - d + zs, zs) + c]
        for e, p in enumerate(item_peers):
            across[d, e] = send(block, block, xy_s.at[d, e], xy_r.at[d, e], (u, p))
        pending.append(send(block, block, sib_s.at[d, items - 1], sib_r.at[d, items - 1], sibling))
    for d in range(zs):
        shard = 2 * lax.rem(z - d + zs, zs) + c
        for e in range(items - 1):
            across[d, e].wait_recv()
            block = x_out.at[lax.rem(i - e - 1 + items, items), :, shard]
            pending.append(send(block, block, sib_s.at[d, e], sib_r.at[d, e], sibling))
    for copy in crossing + list(across.values()):
        copy.wait_send()
    for copy in pending:
        copy.wait()
    keep.wait()


def gather_items(users, items, piece):
    blocks, part, rank = piece.shape
    zs = users // 2
    dma = pltpu.SemaphoreType.DMA
    return pl.pallas_call(
        functools.partial(gather_items_kernel, users, items),
        out_shape=jax.ShapeDtypeStruct((items, blocks, users, part, rank), jnp.float32),
        in_specs=[ANY],
        out_specs=ANY,
        scratch_shapes=[dma((zs,)), dma((zs,))] + [dma((zs, items))] * 4 + [dma],
        compiler_params=pltpu.CompilerParams(
            collective_id=1, has_side_effects=True, vmem_limit_bytes=16 * 2**20
        ),
        name="gather_items",
    )(piece)


def gather_held_kernel(users, items, f_ref, f_out, s_sem, r_sem, local):
    i, u, z, c = place(users, items)
    item_peers = [lax.rem(i + e, items) for e in range(1, items)]
    greet([(u, p) for p in item_peers])
    own = f_out.at[:, i]
    copies = [send(f_ref, own, s_sem.at[e], r_sem.at[e], (u, p)) for e, p in enumerate(item_peers)]
    keep = pltpu.make_async_copy(f_ref, own, local)
    keep.start()
    for copy in copies:
        copy.wait()
    keep.wait()


def gather_held(users, items, piece):
    blocks, part, rank = piece.shape
    dma = pltpu.SemaphoreType.DMA
    return pl.pallas_call(
        functools.partial(gather_held_kernel, users, items),
        out_shape=jax.ShapeDtypeStruct((blocks, items, part, rank), jnp.float32),
        in_specs=[ANY],
        out_specs=ANY,
        scratch_shapes=[dma((items,)), dma((items,)), dma],
        compiler_params=pltpu.CompilerParams(
            collective_id=2, has_side_effects=True, vmem_limit_bytes=16 * 2**20
        ),
        name="gather_held",
    )(piece)


def slot_codes(joined, named, counts, per_owner):
    slots = joined.shape[1]
    live = jnp.arange(slots, dtype=jnp.int32)[None, :] < counts[:, None]
    return jnp.where(live, joined * per_owner + named, -1).reshape(1, -1)


def shards(user_factors, item_factors, tile_user, tile_item, tile_count, tile_conf,
           held_user, held_item, held_count, held_conf):
    users, items = lax.axis_size("user"), lax.axis_size("item")
    width = tile_conf.shape[-1]
    rank = user_factors.shape[1]
    user_blocks = user_factors.shape[0] // width
    item_blocks = item_factors.shape[0] // width
    held_blocks = 2
    u = lax.axis_index("user")
    i = lax.axis_index("item")

    codes = slot_codes(tile_item[0, 0], tile_user[0, 0], tile_count[0, 0], user_blocks)
    held_codes = slot_codes(held_user[0, 0], held_item[0, 0], held_count[0, 0], item_blocks)
    slots, held_slots = codes.shape[1], held_codes.shape[1]
    lanes = -(-max(slots, held_slots) // 128) * 128
    meta = jnp.concatenate([
        jnp.pad(codes, ((0, 0), (0, lanes - slots))),
        jnp.pad(held_codes, ((0, 0), (0, lanes - held_slots))),
        jnp.zeros((6, lanes), jnp.int32),
    ], axis=0)
    conf = tile_conf.reshape(-1, width, width)
    held = held_conf.reshape(-1, width, width)
    table, tiles, held_tiles, user_meta, item_meta = spread(users, items, user_factors, conf, held, meta)

    part = width // users
    start = lax.dynamic_index_in_dim(
        item_factors.reshape(item_blocks, users, part, rank), u, axis=1, keepdims=False
    ).reshape(-1, rank)
    own = solve(user_meta[:, 0, :slots], table.reshape(-1, rank), tiles, item_blocks * part, users, start)
    whole = gather_items(users, items, own.reshape(item_blocks, part, rank))
    new_items = lax.dynamic_index_in_dim(whole, i, axis=0, keepdims=False).reshape(-1, rank)

    held_part = width // items
    folded = solve(item_meta[:, 1, :held_slots], whole.reshape(-1, rank), held_tiles, held_blocks * held_part, items)
    folded_users = gather_held(users, items, folded.reshape(held_blocks, held_part, rank))
    return new_items, folded_users.reshape(-1, rank)


def solution(mesh):
    in_specs = (
        P("user", None),
        P("item", None),
        P("item", "user", None, None),
        P("item", "user", None, None),
        P("item", "user", None),
        P("item", "user", None, None, None, None),
        P("user", "item", None, None),
        P("user", "item", None, None),
        P("user", "item", None),
        P("user", "item", None, None, None, None),
    )
    out_specs = (P("item", None), P("user", None))
    return jax.shard_map(shards, mesh=mesh, in_specs=in_specs, out_specs=out_specs, check_vma=False)
```

time: 471 us -> 86.7 us (0.18); the launches traced: 462 us -> 86.4 us
  waiting for transfers between devices: 375 us -> 0 us
  Pallas kernels: 0 us -> 76.5 us
  matrix products: 46 us -> 0 us
  between operations: 15 us -> 0.71 us
  local copies, waits for them, and re-layouts: 20.1 us -> 6.22 us
    psum x6 -> x0, waiting for transfers between devices: 296 us -> none  [the longest x3 167 us: user_total(): return lax.psum(partial_value, 'user')]
    all_gather x2 -> x0, waiting for transfers between devices: 77.9 us -> none  [the longest x1 44.1 us: shards(): whole_users = lax.all_gather(user_factors, 'user', axis=0, tiled=True)]
    pallas_call x0 -> x5, Pallas kernels: none -> 76.5 us  [the longest x1 30.9 us: spread(): pl.pallas_call(functools.partial(spread_kernel, users, items), out_shape=...]
    dot_general x26 -> x0, matrix products: 46 us -> none  [the longest x3 9.55 us: item_terms(): jnp.einsum('tuk,tik->tui', factors, picked, precision=highest) * weights]
    gather x7 -> x0, local copies, waits for them, and re-layouts: 14.4 us -> none  [the longest x3 7.13 us: item_terms(): picked = vector[positions]]
  transfers between devices with their start and end apart: 8 -> 0, of which waited for: 8 -> 0; matrix products, arithmetic and copies ran while one was open for 2% -> 0% of each run, Pallas kernels for 0% -> 0%
where the time goes in v1:
time: 86.7 us; the launch traced here: 86.4 us
  Pallas kernels  76.5 us (88%)
  local copies, waits for them, and re-layouts  6.22 us (7%)
  other arithmetic  2.94 us (3%)
    pallas_call x1, Pallas kernels, spread(): pl.pallas_call(functools.partial(spread_kernel, users, items), out_shape=...  30.9 us
    pallas_call x1, Pallas kernels, gather_items(): pl.pallas_call(functools.partial(gather_items_kernel, users, items), out_...  20.8 us
    pallas_call x2, Pallas kernels, solve(): pl.pallas_call(functools.partial(solve_kernel, warm, by_owner), out_shape...  18.1 us
    pallas_call x1, Pallas kernels, gather_held(): pl.pallas_call(functools.partial(gather_held_kernel, users, items), out_s...  6.67 us
    unnamed x9, local copies, waits for them, and re-layouts  4.77 us

profile of v1, /device:TPU:0, one launch (start us, length us, event | category | flops | bytes accessed | tf_op | source)
XLA Modules:
  0.0 86.4 jit_solution(8440450009923111899)
XLA Ops:
  0.6 0.0 copy-start
  0.7 1.0 %copy-done = f32[512,256]{1,0:T(8,128)S(1)} copy-done((f32[512,256]{1,0:T(8,128)S(1)}, f32[512,256]{1,0:T(8,128)}, u32[]{:S(2)}) %copy-start) | copy-done | bytes 524312
  1.7 0.7 iota_compare_fusion.1
  2.4 0.1 lt.67
  2.5 0.1 pad.12.clone
  2.6 0.7 multiply_add_fusion.1
  3.3 0.7 iota_compare_fusion
  4.0 0.1 lt.62
  4.1 0.7 multiply_add_fusion
  4.8 0.1 copy.16
  4.9 0.1 add.41
  5.0 0.1 copy.15
  5.1 0.1 add.39
  5.2 0.1 fusion.meta_ref
  5.2 0.0 copy-start.1
  5.2 1.0 %copy-done.1 = f32[512,256]{1,0:T(8,128)S(1)} copy-done((f32[512,256]{1,0:T(8,128)S(1)}, f32[512,256]{1,0:T(8,128)}, u32[]{:S(2)}) %copy-start.1) | copy-done | bytes 524312
  6.3 0.0 copy-start.2
  6.3 1.0 %copy-done.2 = bf16[1,1,8,2,128,128]{5,4,3,2,1,0:T(8,128)(2,1)S(1)} copy-done((bf16[1,1,8,2,128,128]{5,4,3,2,1,0:T(8,128)(2,1)S(1)}, bf16[1,1,8,2,128,128]{5,4,3,2,1,0:T(8,128)(2,1)}, u32[]{:S(2)}) %copy-start.2) | copy-done | bytes 524312
  7.3 0.0 copy-start.3
  7.3 0.9 %copy-done.3 = bf16[1,1,4,2,128,128]{5,4,3,2,1,0:T(8,128)(2,1)S(1)} copy-done((bf16[1,1,4,2,128,128]{5,4,3,2,1,0:T(8,128)(2,1)S(1)}, bf16[1,1,4,2,128,128]{5,4,3,2,1,0:T(8,128)(2,1)}, u32[]{:S(2)}) %copy-start.3) | copy-done | bytes 262168
  8.3 30.9 %spread_inputs.1 = (f32[8,4,128,256]{3,2,1,0:T(8,128)S(1)}, bf16[8,256,128]{2,1,0:T(8,128)(2,1)S(1)}, bf16[4,256,128]{2,1,0:T(8,128)(2,1)S(1)}, s32[8,8,128]{2,1,0:T(8,128)S(1)}, s32[4,8,128]{2,1,0:T(8,128)S(1)}) custom-call(f32[4,128,256]{2,1,0:T(8,128)S(1)} %bitcast.23, bf16[16,128,128]{2,1,0:T(8,128)(2,1)S(1)} %bitcast.24, ...), custom_call_target="tpu_custom_call" | custom-call | tf_op jit(solution)/shard_map/spread_inputs/pallas_call | solution.py:120
  39.2 12.7 %solve_items.1 = f32[64,256]{1,0:T(8,128)S(1)} custom-call(s32[8,16]{1,0:T(8,128)S(1)} %bitcast.29, f32[4096,256]{1,0:T(8,128)S(1)} %bitcast.21, bf16[8,256,128]{2,1,0:T(8,128)(2,1)S(1)} %get-tuple-element.9.tiles_ref, f32[64,256]{1,0:T(8,128)S(1)} %bitcast.26), custom_call_target="tpu_custom_call" | custom-call | tf_op jit(solution)/shard_map/solve_items/pallas_call | solution.py:245
  51.9 20.8 %gather_items.1 = f32[4,4,8,16,256]{4,3,2,1,0:T(8,128)S(1)} custom-call(f32[4,16,256]{2,1,0:T(8,128)S(1)} %bitcast.25), custom_call_target="tpu_custom_call" | custom-call | tf_op jit(solution)/shard_map/gather_items/pallas_call | solution.py:301
  72.7 5.4 %solve_held.1 = f32[64,256]{1,0:T(8,128)S(1)} custom-call(s32[4,8]{1,0:T(4,128)S(1)} %bitcast.30, f32[2048,256]{1,0:T(8,128)S(1)} %bitcast.20, bf16[4,256,128]{2,1,0:T(8,128)(2,1)S(1)} %get-tuple-element.11.tiles_ref), custom_call_target="tpu_custom_call" | custom-call | tf_op jit(solution)/shard_map/solve_held/pallas_call | solution.py:245
  78.2 6.7 %gather_held.1 = f32[2,4,32,256]{3,2,1,0:T(8,128)S(1)} custom-call(f32[2,32,256]{2,1,0:T(8,128)S(1)} %bitcast.28), custom_call_target="tpu_custom_call" | custom-call | tf_op jit(solution)/shard_map/gather_held/pallas_call | solution.py:330
  84.8 0.8 constant_dynamic-slice_fusion
  85.7 0.7 copy.20
  (6 shorter events, 0.0 us)
Async XLA Ops:
  0.6 1.0 %copy-start = (f32[512,256]{1,0:T(8,128)S(1)}, f32[512,256]{1,0:T(8,128)}, u32[]{:S(2)}) copy-start(f32[512,256]{1,0:T(8,128)} %param.11) | copy-start | bytes 1572868
  5.2 1.0 %copy-start.1 = (f32[512,256]{1,0:T(8,128)S(1)}, f32[512,256]{1,0:T(8,128)}, u32[]{:S(2)}) copy-start(f32[512,256]{1,0:T(8,128)} %param.10) | copy-start | bytes 1572868
  6.3 1.0 %copy-start.2 = (bf16[1,1,8,2,128,128]{5,4,3,2,1,0:T(8,128)(2,1)S(1)}, bf16[1,1,8,2,128,128]{5,4,3,2,1,0:T(8,128)(2,1)}, u32[]{:S(2)}) copy-start(bf16[1,1,8,2,128,128]{5,4,3,2,1,0:T(8,128)(2,1)} %param.15) | copy-start | bytes 1572868
  7.3 0.9 %copy-start.3 = (bf16[1,1,4,2,128,128]{5,4,3,2,1,0:T(8,128)(2,1)S(1)}, bf16[1,1,4,2,128,128]{5,4,3,2,1,0:T(8,128)(2,1)}, u32[]{:S(2)}) copy-start(bf16[1,1,4,2,128,128]{5,4,3,2,1,0:T(8,128)(2,1)} %param.19) | copy-start | bytes 786436

commit v2 on v0

v2 whole, which is shorter than its diff:
```python
import functools

import jax
import jax.numpy as jnp
from jax import lax
from jax.experimental import pallas as pl
from jax.experimental.pallas import tpu as pltpu
from jax.sharding import PartitionSpec as P

ITERS = 2
RIDGE = 1.0
EPS = 1e-6
MESH = pl.DeviceIdType.MESH
ANY = pl.BlockSpec(memory_space=pl.ANY)
VMEM = pl.BlockSpec(memory_space=pltpu.VMEM)
HBM = pl.BlockSpec(memory_space=pltpu.HBM)
SMEM = pl.BlockSpec(memory_space=pltpu.SMEM)


def place(users, items):
    u = lax.axis_index("user")
    return lax.axis_index("item"), u, u // 2, lax.rem(u, 2)


def greet(devices):
    for device in devices:
        pl.semaphore_signal(pltpu.get_barrier_semaphore(), inc=1, device_id=device, device_id_type=MESH)


def await_greetings(devices):
    pl.semaphore_wait(pltpu.get_barrier_semaphore(), len(devices))


def send(src, dst, send_sem, recv_sem, device):
    copy = pltpu.make_async_remote_copy(
        src_ref=src, dst_ref=dst, send_sem=send_sem, recv_sem=recv_sem, device_id=device, device_id_type=MESH
    )
    copy.start()
    return copy


def pack_rows(tile_of, out, slots, peers):
    rows = out.shape[1] // slots
    group = max(1, 16 // rows)
    for first in range(0, slots, group):
        tiles = [tile_of(first + k) for k in range(group)]
        for p in range(peers):
            part = [t[p * rows:(p + 1) * rows] for t in tiles]
            part = part[0] if group == 1 else jnp.concatenate(part, axis=0)
            out[p, first * rows:(first + group) * rows, :] = part.astype(out.dtype)


def halves(value):
    high = value.astype(jnp.bfloat16)
    return high, (value - high.astype(jnp.float32)).astype(jnp.bfloat16)


def dot(a, b, contract):
    return lax.dot_general(a, b, (((1,), (contract,)), ((), ())), preferred_element_type=jnp.float32)


def product(value, high, low, contract):
    n = value.shape[0]
    top, bottom = halves(value)
    both = dot(jnp.concatenate([top, bottom], axis=0), high, contract)
    return both[:n] + both[n:] + dot(top, low, contract)


def describe(joined, named, counts, lanes):
    at = lax.broadcasted_iota(jnp.int32, (joined.shape[0], lanes), 1)
    cap = joined.shape[1]
    out = jnp.where(at == 2 * cap, counts, 0)
    for k in range(cap):
        out = jnp.where(at == k, joined[:, k:k + 1], out)
        out = jnp.where(at == cap + k, named[:, k:k + 1], out)
    return out


def spread_kernel(users, items, y_hbm, conf_hbm, held_hbm, ti_ref, tu_ref, tc_ref, hu_ref, hi_ref, hc_ref,
                  y_out, c_out, h_out, mu_out, mi_out, y_ref, conf_ref, held_ref, y_send, c_send, h_send, mu_send, mi_send,
                  z_s, z_r, xy_s, xy_r, sib_s, sib_r, own_s, own_r,
                  c_s, c_r, h_s, h_r, mu_s, mu_r, mi_s, mi_r, local):
    zs = users // 2
    i, u, z, c = place(users, items)
    sibling = (2 * z + 1 - c, i)
    quarter = y_send.shape[2]
    user_peers = [lax.rem(u + k, users) for k in range(1, users)]
    item_peers = [lax.rem(i + e, items) for e in range(1, items)]
    neighbours = [(p, i) for p in user_peers] + [(u, p) for p in item_peers]
    loads = [
        pltpu.make_async_copy(y_hbm, y_ref, local.at[5]),
        pltpu.make_async_copy(held_hbm, held_ref, local.at[6]),
        pltpu.make_async_copy(conf_hbm, conf_ref, local.at[7]),
    ]
    for load in loads:
        load.start()
    greet(neighbours)
    mu_send[...] = jnp.zeros_like(mu_send)
    mi_send[...] = jnp.zeros_like(mi_send)
    mu_send[0:users, :] = describe(ti_ref[...], tu_ref[...], tc_ref[...], mu_send.shape[1])
    mi_send[0:items, :] = describe(hu_ref[...], hi_ref[...], hc_ref[...], mi_send.shape[1])
    loads[0].wait()
    for q in range(items):
        top, bottom = halves(y_ref[q * quarter:(q + 1) * quarter, :])
        y_send[q, 0] = top
        y_send[q, 1] = bottom
    await_greetings(neighbours)

    pending = []
    crossing = []
    for d in range(1, zs):
        peer = 2 * lax.rem(z + d, zs) + c
        crossing.append(send(y_send.at[i], y_out.at[u, i], z_s.at[d], z_r.at[d], (peer, i)))
    pending.append(send(y_send, y_out.at[u], own_s, own_r, sibling))
    keep = [pltpu.make_async_copy(y_send, y_out.at[u], local.at[0])]
    keep[0].start()

    held_slots = held_ref.shape[0]
    loads[1].wait()
    pack_rows(lambda s: held_ref[s].astype(jnp.float32), h_send, held_slots, items)
    for e, p in enumerate(item_peers):
        pending.append(send(h_send.at[p], h_out.at[i], h_s.at[e], h_r.at[e], (u, p)))
        pending.append(send(mi_send, mi_out.at[i], mi_s.at[e], mi_r.at[e], (u, p)))
    for k, p in enumerate(user_peers):
        pending.append(send(mu_send, mu_out.at[u], mu_s.at[k], mu_r.at[k], (p, i)))
    slots = conf_ref.shape[0]
    loads[2].wait()
    pack_rows(lambda s: conf_ref[s].astype(jnp.float32).T, c_send, slots, users)
    keep.append(pltpu.make_async_copy(c_send.at[u], c_out.at[u], local.at[1]))
    keep.append(pltpu.make_async_copy(h_send.at[i], h_out.at[i], local.at[2]))
    keep.append(pltpu.make_async_copy(mu_send, mu_out.at[u], local.at[3]))
    keep.append(pltpu.make_async_copy(mi_send, mi_out.at[i], local.at[4]))
    for copy in keep[1:]:
        copy.start()

    across = {}
    for d in range(1, zs):
        crossing[d - 1].wait_recv()
        shard = 2 * lax.rem(z - d + zs, zs) + c
        block = y_out.at[shard, i]
        for e, p in enumerate(item_peers):
            across[d, e] = send(block, block, xy_s.at[d, e], xy_r.at[d, e], (u, p))
        pending.append(send(block, block, sib_s.at[d, items - 1], sib_r.at[d, items - 1], sibling))
    for k, p in enumerate(user_peers):
        pending.append(send(c_send.at[p], c_out.at[u], c_s.at[k], c_r.at[k], (p, i)))
    for d in range(1, zs):
        shard = 2 * lax.rem(z - d + zs, zs) + c
        for e in range(items - 1):
            across[d, e].wait_recv()
            block = y_out.at[shard, lax.rem(i - e - 1 + items, items)]
            pending.append(send(block, block, sib_s.at[d, e], sib_r.at[d, e], sibling))
    for copy in crossing + list(across.values()):
        copy.wait_send()
    for copy in pending:
        copy.wait()
    for copy in keep:
        copy.wait()


def padded(rows):
    return -(-rows // 8) * 8


def spread(users, items, factors, conf, held, lists, held_lists):
    rows, rank = factors.shape
    slots, width = conf.shape[0], conf.shape[1]
    held_slots = held.shape[0]
    zs = users // 2
    y_piece = (2, rows // items, rank)
    c_piece = (slots * width // users, width)
    h_piece = (held_slots * width // items, width)
    mu_piece, mi_piece = (padded(users), 128), (padded(items), 128)
    dma = pltpu.SemaphoreType.DMA
    bf16, f32 = jnp.bfloat16, jnp.float32
    return pl.pallas_call(
        functools.partial(spread_kernel, users, items),
        out_shape=[
            jax.ShapeDtypeStruct((users, items) + y_piece, bf16),
            jax.ShapeDtypeStruct((users,) + c_piece, bf16),
            jax.ShapeDtypeStruct((items,) + h_piece, bf16),
            jax.ShapeDtypeStruct((users,) + mu_piece, jnp.int32),
            jax.ShapeDtypeStruct((items,) + mi_piece, jnp.int32),
        ],
        in_specs=[HBM] * 3 + [VMEM] * 6,
        out_specs=[ANY] * 5,
        scratch_shapes=[
            pltpu.VMEM((rows, rank), f32),
            pltpu.VMEM(conf.shape, bf16),
            pltpu.VMEM(held.shape, bf16),
            pltpu.VMEM((items,) + y_piece, bf16),
            pltpu.VMEM((users,) + c_piece, bf16),
            pltpu.VMEM((items,) + h_piece, bf16),
            pltpu.VMEM(mu_piece, jnp.int32),
            pltpu.VMEM(mi_piece, jnp.int32),
            dma((zs,)), dma((zs,)), dma((zs, items)), dma((zs, items)), dma((zs, items)), dma((zs, items)),
            dma, dma, dma((users,)), dma((users,)), dma((items,)), dma((items,)),
            dma((users,)), dma((users,)), dma((items,)), dma((items,)), dma((8,)),
        ],
        compiler_params=pltpu.CompilerParams(
            collective_id=0, has_side_effects=True, vmem_limit_bytes=16 * 2**20
        ),
        name="spread_inputs",
    )(factors, conf, held, *lists, *held_lists)


def place_kernel(item_blocks, user_blocks, mu_ref, mi_ref, c_ref, h_ref, w_ref, right_ref, v_ref, held_right_ref):
    def scatter(lists, tiles, weight, right, per_owner, part):
        blocks, rows, width = weight.shape
        sources, piece = tiles.shape[0], tiles.shape[1]
        owners = blocks // per_owner
        slots = piece // part
        cap = slots // owners
        weight[...] = jnp.ones_like(weight)
        right[...] = jnp.zeros_like(right)

        def source_step(source, carry):
            for owner in range(owners):
                for k in range(cap):
                    @pl.when(k < lists[source, owner, 2 * cap])
                    def _():
                        block = owner * per_owner + lists[source, owner, cap + k]
                        at = pl.ds(pl.multiple_of(lists[source, owner, k] * part, part), part)
                        first = (owner * cap + k) * part
                        tile = tiles[source, first:first + part, :].astype(jnp.float32)
                        weight[block, at, :] += tile
                        right[block, at, :] += tile + 1.0
            return carry

        lax.fori_loop(0, sources, source_step, 0)

    scatter(mu_ref, c_ref, w_ref, right_ref, user_blocks, w_ref.shape[1] // item_blocks)
    scatter(mi_ref, h_ref, v_ref, held_right_ref, item_blocks, h_ref.shape[2] // h_ref.shape[0])


def place_tiles(item_blocks, user_blocks, held_blocks, user_lists, item_lists, tiles, held_tiles):
    users, items, width = tiles.shape[0], held_tiles.shape[0], tiles.shape[2]
    item_side = jax.ShapeDtypeStruct((users * user_blocks, item_blocks * width // users, width), jnp.float32)
    held_side = jax.ShapeDtypeStruct((items * item_blocks, held_blocks * width // items, width), jnp.float32)
    return pl.pallas_call(
        functools.partial(place_kernel, item_blocks, user_blocks),
        out_shape=[item_side, item_side, held_side, held_side],
        in_specs=[SMEM, SMEM, VMEM, VMEM],
        out_specs=[VMEM] * 4,
        compiler_params=pltpu.CompilerParams(vmem_limit_bytes=16 * 2**20),
        name="place_tiles",
    )(user_lists, item_lists, tiles, held_tiles)


def conjugate(chunk_of, weight, right, x, rows, rank, chunks):
    per_chunk = weight.shape[0] // chunks

    def wide(ref, n):
        return jnp.concatenate([ref[n * per_chunk + k] for k in range(per_chunk)], axis=1)

    def sweep(coefficients):
        def step(n, total):
            top, bottom = chunk_of(n)
            return total + product(coefficients(n, top, bottom), top, bottom, 0)

        return lax.fori_loop(0, chunks, step, jnp.zeros((rows, rank), jnp.float32), unroll=2)

    def operator(vector):
        return sweep(lambda n, top, bottom: product(vector, top, bottom, 1) * wide(weight, n)) + RIDGE * vector

    if x is None:
        x = jnp.zeros((rows, rank), jnp.float32)
        residual = sweep(lambda n, top, bottom: wide(right, n))
    else:
        residual = sweep(
            lambda n, top, bottom: wide(right, n) - product(x, top, bottom, 1) * wide(weight, n)
        ) - RIDGE * x
    direction = residual
    norm = jnp.sum(residual * residual, axis=1, keepdims=True)
    for iteration in range(ITERS):
        image = operator(direction)
        alpha = norm / (jnp.sum(direction * image, axis=1, keepdims=True) + EPS)
        x = x + alpha * direction
        if iteration + 1 < ITERS:
            residual = residual - alpha * image
            following = jnp.sum(residual * residual, axis=1, keepdims=True)
            direction = residual + following / (norm + EPS) * direction
            norm = following
    return x


def merge_rows(value):
    if value.shape[-2] % 16:
        return value.astype(jnp.float32).reshape(-1, value.shape[-1]).astype(value.dtype)
    return value.reshape(-1, value.shape[-1])


def solve_kernel(users, items, y_ref, start_ref, w_ref, right_ref, v_ref, held_right_ref,
                 new_ref, fold_ref, x_all, x_own, f_own,
                 z_s, z_r, xy_s, xy_r, sib_s, sib_r, f_s, f_r, local):
    zs = users // 2
    i, u, z, c = place(users, items)
    sibling = (2 * z + 1 - c, i)
    z_peers = [2 * lax.rem(z + d, zs) + c for d in range(1, zs)]
    item_peers = [lax.rem(i + e, items) for e in range(1, items)]
    neighbours = [(p, i) for p in z_peers] + [(u, p) for p in item_peers] + [sibling]
    greet(neighbours)

    _, blocks, part, rank = x_own.shape
    x = conjugate(
        lambda n: (merge_rows(y_ref[n, :, 0]), merge_rows(y_ref[n, :, 1])),
        w_ref, right_ref, start_ref[...], blocks * part, rank, users,
    )
    top, bottom = halves(x)
    x_own[0] = top.astype(jnp.float32).reshape(blocks, part, rank).astype(jnp.bfloat16)
    x_own[1] = bottom.astype(jnp.float32).reshape(blocks, part, rank).astype(jnp.bfloat16)
    await_greetings(neighbours)

    crossing, across, pending = [], {}, []
    own = x_all.at[i, :, :, u]
    for d, p in enumerate(z_peers):
        crossing.append(send(x_own, own, z_s.at[d], z_r.at[d], (p, i)))
    for e, p in enumerate(item_peers):
        across[0, e] = send(x_own, own, xy_s.at[0, e], xy_r.at[0, e], (u, p))
    pending.append(send(x_own, own, sib_s.at[0, items - 1], sib_r.at[0, items - 1], sibling))
    keep = pltpu.make_async_copy(x_own, own, local.at[0])
    keep.start()
    for d in range(1, zs):
        crossing[d - 1].wait_recv()
        block = x_all.at[i, :, :, 2 * lax.rem(z - d + zs, zs) + c]
        for e, p in enumerate(item_peers):
            across[d, e] = send(block, block, xy_s.at[d, e], xy_r.at[d, e], (u, p))
        pending.append(send(block, block, sib_s.at[d, items - 1], sib_r.at[d, items - 1], sibling))
    for d in range(zs):
        shard = 2 * lax.rem(z - d + zs, zs) + c
        for e in range(items - 1):
            across[d, e].wait_recv()
            block = x_all.at[lax.rem(i - e - 1 + items, items), :, :, shard]
            pending.append(send(block, block, sib_s.at[d, e], sib_r.at[d, e], sibling))
    for copy in crossing + list(across.values()):
        copy.wait_send()
    for copy in pending:
        copy.wait()
    keep.wait()

    new_ref[...] = merge_rows(x_all[i, 0]).astype(jnp.float32) + merge_rows(x_all[i, 1]).astype(jnp.float32)
    held_blocks, held_part, _ = f_own.shape
    folded = conjugate(
        lambda n: (merge_rows(x_all[n, 0]), merge_rows(x_all[n, 1])),
        v_ref, held_right_ref, None, held_blocks * held_part, rank, items,
    )
    f_own[...] = folded.reshape(held_blocks, held_part, rank)
    mine = fold_ref.at[:, i]
    copies = [send(f_own, mine, f_s.at[e], f_r.at[e], (u, p)) for e, p in enumerate(item_peers)]
    last = pltpu.make_async_copy(f_own, mine, local.at[1])
    last.start()
    for copy in copies:
        copy.wait()
    last.wait()


def solve(users, items, table, start, item_blocks, held_blocks, width, *weights):
    rank = start.shape[1]
    part, held_part = width // users, width // items
    dma = pltpu.SemaphoreType.DMA
    return pl.pallas_call(
        functools.partial(solve_kernel, users, items),
        out_shape=[
            jax.ShapeDtypeStruct((item_blocks * width, rank), jnp.float32),
            jax.ShapeDtypeStruct((held_blocks, items, held_part, rank), jnp.float32),
        ],
        in_specs=[VMEM] * 6,
        out_specs=[VMEM, VMEM],
        scratch_shapes=[
            pltpu.VMEM((items, 2, item_blocks, users, part, rank), jnp.bfloat16),
            pltpu.VMEM((2, item_blocks, part, rank), jnp.bfloat16),
            pltpu.VMEM((held_blocks, held_part, rank), jnp.float32),
            dma((zs := users // 2,)), dma((zs,)),
        ] + [dma((zs, items))] * 4 + [dma((items,)), dma((items,)), dma((2,))],
        compiler_params=pltpu.CompilerParams(
            collective_id=1, has_side_effects=True, vmem_limit_bytes=48 * 2**20
        ),
        name="solve_and_gather",
    )(table, start, *weights)


def shards(user_factors, item_factors, tile_user, tile_item, tile_count, tile_conf,
           held_user, held_item, held_count, held_conf):
    users, items = lax.axis_size("user"), lax.axis_size("item")
    width = tile_conf.shape[-1]
    rank = user_factors.shape[1]
    user_blocks = user_factors.shape[0] // width
    item_blocks = item_factors.shape[0] // width
    held_blocks = 2
    u = lax.axis_index("user")

    conf = tile_conf.reshape(-1, width, width)
    held = held_conf.reshape(-1, width, width)
    lists = (tile_item[0, 0], tile_user[0, 0], tile_count.reshape(-1, 1))
    held_lists = (held_user[0, 0], held_item[0, 0], held_count.reshape(-1, 1))
    table, tiles, held_tiles, user_lists, item_lists = spread(
        users, items, user_factors, conf, held, lists, held_lists
    )
    weights = place_tiles(item_blocks, user_blocks, held_blocks, user_lists, item_lists, tiles, held_tiles)
    start = lax.dynamic_index_in_dim(
        item_factors.reshape(item_blocks, users, width // users, rank), u, axis=1, keepdims=False
    ).reshape(-1, rank)
    new_items, folded = solve(users, items, table, start, item_blocks, held_blocks, width, *weights)
    return new_items, folded.reshape(-1, rank)


def solution(mesh):
    in_specs = (
        P("user", None),
        P("item", None),
        P("item", "user", None, None),
        P("item", "user", None, None),
        P("item", "user", None),
        P("item", "user", None, None, None, None),
        P("user", "item", None, None),
        P("user", "item", None, None),
        P("user", "item", None),
        P("user", "item", None, None, None, None),
    )
    out_specs = (P("item", None), P("user", None))
    return jax.shard_map(shards, mesh=mesh, in_specs=in_specs, out_specs=out_specs, check_vma=False)
```

time: 471 us -> 89.7 us (0.19); the launches traced: 462 us -> 89.3 us
  waiting for transfers between devices: 375 us -> 0 us
  Pallas kernels: 0 us -> 75.7 us
  matrix products: 46 us -> 0 us
  between operations: 15 us -> 0.7 us
  local copies, waits for them, and re-layouts: 20.1 us -> 12.9 us
  other arithmetic: 5.18 us -> 0 us
    psum x6 -> x0, waiting for transfers between devices: 296 us -> none  [the longest x3 167 us: user_total(): return lax.psum(partial_value, 'user')]
    all_gather x2 -> x0, waiting for transfers between devices: 77.9 us -> none  [the longest x1 44.1 us: shards(): whole_users = lax.all_gather(user_factors, 'user', axis=0, tiled=True)]
    pallas_call x0 -> x3, Pallas kernels: none -> 75.7 us  [the longest x1 41.2 us: solve(): pl.pallas_call(functools.partial(solve_kernel, users, items), out_shape=[...]
    dot_general x26 -> x0, matrix products: 46 us -> none  [the longest x3 9.55 us: item_terms(): jnp.einsum('tuk,tik->tui', factors, picked, precision=highest) * weights]
    gather x7 -> x0, local copies, waits for them, and re-layouts: 14.4 us -> none  [the longest x3 7.13 us: item_terms(): picked = vector[positions]]
    unnamed x30 -> x16, local copies, waits for them, and re-layouts: 0.92 us -> 8.3 us
  transfers between devices with their start and end apart: 8 -> 0, of which waited for: 8 -> 0; matrix products, arithmetic and copies ran while one was open for 2% -> 0% of each run, Pallas kernels for 0% -> 0%
where the time goes in v2:
time: 89.7 us; the launch traced here: 89.3 us
  Pallas kernels  75.7 us (84%)
  local copies, waits for them, and re-layouts  12.9 us (14%)
    pallas_call x1, Pallas kernels, solve(): pl.pallas_call(functools.partial(solve_kernel, users, items), out_shape=[...  41.2 us
    pallas_call x1, Pallas kernels, spread(): pl.pallas_call(functools.partial(spread_kernel, users, items), out_shape=...  31 us
    unnamed x16, local copies, waits for them, and re-layouts  8.3 us
    pallas_call x1, Pallas kernels, place_tiles(): pl.pallas_call(functools.partial(place_kernel, item_blocks, user_blocks),...  3.5 us

profile of v2, /device:TPU:0, one launch (start us, length us, event | category | flops | bytes accessed | tf_op | source)
XLA Modules:
  0.0 89.3 jit_solution(12745651279151584921)
XLA Ops:
  0.6 0.0 copy-start
  0.6 0.8 copy.12.ti_ref
  1.5 0.8 copy.13.tu_ref
  2.2 0.7 copy.14.tc_ref
  2.9 0.8 copy.15.hu_ref
  3.7 0.8 copy.16.hi_ref
  4.5 0.7 copy.17.hc_ref
  5.2 0.0 copy-start.4
  5.2 1.0 %copy-done.4 = f32[512,256]{1,0:T(8,128)S(1)} copy-done((f32[512,256]{1,0:T(8,128)S(1)}, f32[512,256]{1,0:T(8,128)}, u32[]{:S(2)}) %copy-start.4) | copy-done | bytes 524312
  6.3 0.0 copy-start.5
  6.3 1.0 %copy-done.5 = bf16[1,1,8,2,128,128]{5,4,3,2,1,0:T(8,128)(2,1)S(1)} copy-done((bf16[1,1,8,2,128,128]{5,4,3,2,1,0:T(8,128)(2,1)S(1)}, bf16[1,1,8,2,128,128]{5,4,3,2,1,0:T(8,128)(2,1)}, u32[]{:S(2)}) %copy-start.5) | copy-done | bytes 524312
  7.3 0.0 copy-start.6
  7.3 0.9 %copy-done.6 = bf16[1,1,4,2,128,128]{5,4,3,2,1,0:T(8,128)(2,1)S(1)} copy-done((bf16[1,1,4,2,128,128]{5,4,3,2,1,0:T(8,128)(2,1)S(1)}, bf16[1,1,4,2,128,128]{5,4,3,2,1,0:T(8,128)(2,1)}, u32[]{:S(2)}) %copy-start.6) | copy-done | bytes 262168
  8.2 31.0 %spread_inputs.1 = (bf16[8,4,2,128,256]{4,3,2,1,0:T(8,128)(2,1)S(1)}, bf16[8,256,128]{2,1,0:T(8,128)(2,1)S(1)}, bf16[4,256,128]{2,1,0:T(8,128)(2,1)S(1)}, s32[8,8,128]{2,1,0:T(8,128)S(1)}, s32[4,8,128]{2,1,0:T(8,128)S(1)}) custom-call(f32[512,256]{1,0:T(8,128)S(1)} %copy-done.4, bf16[16,128,128]{2,1,0:T(8,128)(2,1)S(1)} %bitcast.14, ...), custom_call_target="tpu_custom_call" | custom-call | tf_op jit(solution)/shard_map/spread_inputs/pallas_call | solution.py:175
  39.3 0.0 copy-start.1
  39.3 1.9 %copy-done.1 = bf16[8,4,2,128,256]{4,3,2,1,0:T(8,128)(2,1)} copy-done((bf16[8,4,2,128,256]{4,3,2,1,0:T(8,128)(2,1)}, bf16[8,4,2,128,256]{4,3,2,1,0:T(8,128)(2,1)S(1)}, u32[]{:S(2)}) %copy-start.1) | copy-done | bytes 4194328
  41.2 3.5 %place_tiles.1 = (f32[32,64,128]{2,1,0:T(8,128)S(1)}, f32[32,64,128]{2,1,0:T(8,128)S(1)}, f32[16,64,128]{2,1,0:T(8,128)S(1)}, f32[16,64,128]{2,1,0:T(8,128)S(1)}) custom-call(s32[8,8,128]{2,1,0:T(8,128)S(1)} %get-tuple-element.14.mu_ref, s32[4,8,128]{2,1,0:T(8,128)S(1)} %get-tuple-element.15.mi_ref, bf16[8,256,128]{2,1,0:T(8,128)(2,1)S(1)} %get-tuple-element.16.c_ref, ...), custom_call_target="tpu_custom_call" | custom-call | tf_op jit(solution)/shard_map/place_tiles/pallas_call | solution.py:239
  44.7 0.0 copy-start.2
  44.8 0.8 copy-done.2
  45.5 0.0 copy-done
  45.6 0.0 copy-start.3
  45.6 1.0 %copy-done.3 = f32[16,64,128]{2,1,0:T(8,128)S(1)} copy-done((f32[16,64,128]{2,1,0:T(8,128)S(1)}, f32[16,64,128]{2,1,0:T(8,128)}, u32[]{:S(2)}) %copy-start.3) | copy-done | bytes 524312
  46.6 41.2 %solve_and_gather.1 = (f32[512,256]{1,0:T(8,128)S(1)}, f32[2,4,32,256]{3,2,1,0:T(8,128)S(1)}) custom-call(bf16[8,4,2,128,256]{4,3,2,1,0:T(8,128)(2,1)} %copy-done.1, f32[64,256]{1,0:T(8,128)S(1)} %bitcast.15, f32[32,64,128]{2,1,0:T(8,128)S(1)} %get-tuple-element.18.w_ref, f32[32,64,128]{2,1,0:T(8,128)S(1)} %get-tuple-element.19.right_ref, ...), custom_call_target="tpu_custom_call" | custom-call | tf_op jit(solution)/shard_map/solve_and_gather/pallas_call | solution.py:360
  87.8 0.8 copy.22
  88.6 0.7 copy.23
  (1 shorter events, 0.0 us)
Async XLA Ops:
  0.6 44.9 %copy-start = (f32[512,256]{1,0:T(8,128)S(1)}, f32[512,256]{1,0:T(8,128)}, u32[]{:S(2)}) copy-start(f32[512,256]{1,0:T(8,128)} %param.11) | copy-start | bytes 1572868
  5.2 1.0 %copy-start.4 = (f32[512,256]{1,0:T(8,128)S(1)}, f32[512,256]{1,0:T(8,128)}, u32[]{:S(2)}) copy-start(f32[512,256]{1,0:T(8,128)} %y_hbm.1) | copy-start | bytes 1572868
  6.3 1.0 %copy-start.5 = (bf16[1,1,8,2,128,128]{5,4,3,2,1,0:T(8,128)(2,1)S(1)}, bf16[1,1,8,2,128,128]{5,4,3,2,1,0:T(8,128)(2,1)}, u32[]{:S(2)}) copy-start(bf16[1,1,8,2,128,128]{5,4,3,2,1,0:T(8,128)(2,1)} %param.15) | copy-start | bytes 1572868
  7.3 0.9 %copy-start.6 = (bf16[1,1,4,2,128,128]{5,4,3,2,1,0:T(8,128)(2,1)S(1)}, bf16[1,1,4,2,128,128]{5,4,3,2,1,0:T(8,128)(2,1)}, u32[]{:S(2)}) copy-start(bf16[1,1,4,2,128,128]{5,4,3,2,1,0:T(8,128)(2,1)} %param.19) | copy-start | bytes 786436
  39.3 1.9 %copy-start.1 = (bf16[8,4,2,128,256]{4,3,2,1,0:T(8,128)(2,1)}, bf16[8,4,2,128,256]{4,3,2,1,0:T(8,128)(2,1)S(1)}, u32[]{:S(2)}) copy-start(bf16[8,4,2,128,256]{4,3,2,1,0:T(8,128)(2,1)S(1)} %get-tuple-element.13.y_ref) | copy-start | bytes 12582916
  44.7 0.8 copy-start.2
  45.6 1.0 %copy-start.3 = (f32[16,64,128]{2,1,0:T(8,128)S(1)}, f32[16,64,128]{2,1,0:T(8,128)}, u32[]{:S(2)}) copy-start(f32[16,64,128]{2,1,0:T(8,128)} %copy-done.2) | copy-start | bytes 1572868

commit v3 on v2

--- a/solution.py
+++ b/solution.py
@@ -66,14 +66,68 @@
     return both[:n] + both[n:] + dot(top, low, contract)
 
 
-def describe(joined, named, counts, lanes):
-    at = lax.broadcasted_iota(jnp.int32, (joined.shape[0], lanes), 1)
-    cap = joined.shape[1]
-    out = jnp.where(at == 2 * cap, counts, 0)
-    for k in range(cap):
-        out = jnp.where(at == k, joined[:, k:k + 1], out)
-        out = jnp.where(at == cap + k, named[:, k:k + 1], out)
-    return out
+def describe(out, joined, named, counts):
+    cap, owners = joined.shape
+    out[...] = jnp.zeros_like(out)
+    out[0:cap, 0:owners] = joined[...]
+    out[cap:2 * cap, 0:owners] = named[...]
+    out[2 * cap:2 * cap + 1, 0:owners] = counts[...]
+
+
+def exchange(items, u, i, d, block, half, sibling, xy_s, xy_r, sib_s, sib_r, sent, pending):
+    direct, relays = [], []
+
+    def mirror(q, slot):
+        pending.append(send(block(q), block(q), sib_s.at[d, slot], sib_r.at[d, slot], sibling))
+
+    def hop(src, slot, p):
+        copy = send(src, src, xy_s.at[d, slot], xy_r.at[d, slot], (u, p))
+        sent.append(copy)
+        return copy
+
+    if items != 4:
+        def first(src):
+            for e in range(1, items):
+                copy = send(src, block(i), xy_s.at[d, e], xy_r.at[d, e], (u, lax.rem(i + e, items)))
+                direct.append(copy)
+                sent.append(copy)
+            pending.append(send(src, block(i), sib_s.at[d, 0], sib_r.at[d, 0], sibling))
+
+        def second():
+            return None
+
+        def third():
+            for e in range(1, items):
+                direct[e - 1].wait_recv()
+                mirror(lax.rem(i - e + items, items), e)
+
+        return first, second, third
+
+    flip = 1 - 2 * lax.rem(i, 2)
+    beside, behind = i + flip, lax.rem(i + 2, 4)
+    opposite = behind + flip
+
+    def first(src):
+        for slot, p in enumerate((beside, behind)):
+            copy = send(src, block(i), xy_s.at[d, slot], xy_r.at[d, slot], (u, p))
+            direct.append(copy)
+            sent.append(copy)
+        pending.append(send(src, block(i), sib_s.at[d, 3], sib_r.at[d, 3], sibling))
+
+    def second():
+        direct[0].wait_recv()
+        relays.append(hop(half(beside, 0), 3, behind))
+        mirror(beside, 0)
+        direct[1].wait_recv()
+        relays.append(hop(half(behind, 1), 2, beside))
+        mirror(behind, 1)
+
+    def third():
+        for copy in relays:
+            copy.wait_recv()
+        mirror(opposite, 2)
+
+    return first, second, third
 
 
 def spread_kernel(users, items, y_hbm, conf_hbm, held_hbm, ti_ref, tu_ref, tc_ref, hu_ref, hi_ref, hc_ref,
@@ -95,10 +149,8 @@
     for load in loads:
         load.start()
     greet(neighbours)
-    mu_send[...] = jnp.zeros_like(mu_send)
-    mi_send[...] = jnp.zeros_like(mi_send)
-    mu_send[0:users, :] = describe(ti_ref[...], tu_ref[...], tc_ref[...], mu_send.shape[1])
-    mi_send[0:items, :] = describe(hu_ref[...], hi_ref[...], hc_ref[...], mi_send.shape[1])
+    describe(mu_send, ti_ref, tu_ref, tc_ref)
+    describe(mi_send, hu_ref, hi_ref, hc_ref)
     loads[0].wait()
     for q in range(items):
         top, bottom = halves(y_ref[q * quarter:(q + 1) * quarter, :])
@@ -133,32 +185,27 @@
     for copy in keep[1:]:
         copy.start()
 
-    across = {}
+    sent, stages = [], []
+    for d in range(1, zs):
+        shard = 2 * lax.rem(z - d + zs, zs) + c
+        stages.append(exchange(
+            items, u, i, d, lambda q, n=shard: y_out.at[n, q], lambda q, h, n=shard: y_out.at[n, q, h],
+            sibling, xy_s, xy_r, sib_s, sib_r, sent, pending,
+        ))
     for d in range(1, zs):
         crossing[d - 1].wait_recv()
-        shard = 2 * lax.rem(z - d + zs, zs) + c
-        block = y_out.at[shard, i]
-        for e, p in enumerate(item_peers):
-            across[d, e] = send(block, block, xy_s.at[d, e], xy_r.at[d, e], (u, p))
-        pending.append(send(block, block, sib_s.at[d, items - 1], sib_r.at[d, items - 1], sibling))
+        stages[d - 1][0](y_out.at[2 * lax.rem(z - d + zs, zs) + c, i])
     for k, p in enumerate(user_peers):
         pending.append(send(c_send.at[p], c_out.at[u], c_s.at[k], c_r.at[k], (p, i)))
-    for d in range(1, zs):
-        shard = 2 * lax.rem(z - d + zs, zs) + c
-        for e in range(items - 1):
-            across[d, e].wait_recv()
-            block = y_out.at[shard, lax.rem(i - e - 1 + items, items)]
-            pending.append(send(block, block, sib_s.at[d, e], sib_r.at[d, e], sibling))
-    for copy in crossing + list(across.values()):
+    for number in (1, 2):
+        for stage in stages:
+            stage[number]()
+    for copy in crossing + sent:
         copy.wait_send()
     for copy in pending:
         copy.wait()
     for copy in keep:
         copy.wait()
-
-
-def padded(rows):
-    return -(-rows // 8) * 8
 
 
 def spread(users, items, factors, conf, held, lists, held_lists):
@@ -169,7 +216,7 @@
     y_piece = (2, rows // items, rank)
     c_piece = (slots * width // users, width)
     h_piece = (held_slots * width // items, width)
-    mu_piece, mi_piece = (padded(users), 128), (padded(items), 128)
+    mu_piece = mi_piece = (8, 128)
     dma = pltpu.SemaphoreType.DMA
     bf16, f32 = jnp.bfloat16, jnp.float32
     return pl.pallas_call(
@@ -197,7 +244,7 @@
             dma((users,)), dma((users,)), dma((items,)), dma((items,)), dma((8,)),
         ],
         compiler_params=pltpu.CompilerParams(
-            collective_id=0, has_side_effects=True, vmem_limit_bytes=16 * 2**20
+            collective_id=0, has_side_effects=True, vmem_limit_bytes=60 * 2**20
         ),
         name="spread_inputs",
     )(factors, conf, held, *lists, *held_lists)
@@ -216,10 +263,10 @@
         def source_step(source, carry):
             for owner in range(owners):
                 for k in range(cap):
-                    @pl.when(k < lists[source, owner, 2 * cap])
+                    @pl.when(k < lists[source, 2 * cap, owner])
                     def _():
-                        block = owner * per_owner + lists[source, owner, cap + k]
-                        at = pl.ds(pl.multiple_of(lists[source, owner, k] * part, part), part)
+                        block = owner * per_owner + lists[source, cap + k, owner]
+                        at = pl.ds(pl.multiple_of(lists[source, k, owner] * part, part), part)
                         first = (owner * cap + k) * part
                         tile = tiles[source, first:first + part, :].astype(jnp.float32)
                         weight[block, at, :] += tile
@@ -241,7 +288,7 @@
         out_shape=[item_side, item_side, held_side, held_side],
         in_specs=[SMEM, SMEM, VMEM, VMEM],
         out_specs=[VMEM] * 4,
-        compiler_params=pltpu.CompilerParams(vmem_limit_bytes=16 * 2**20),
+        compiler_params=pltpu.CompilerParams(vmem_limit_bytes=60 * 2**20),
         name="place_tiles",
     )(user_lists, item_lists, tiles, held_tiles)
 
@@ -310,28 +357,26 @@
     x_own[1] = bottom.astype(jnp.float32).reshape(blocks, part, rank).astype(jnp.bfloat16)
     await_greetings(neighbours)
 
-    crossing, across, pending = [], {}, []
+    crossing, sent, pending, stages = [], [], [], []
     own = x_all.at[i, :, :, u]
     for d, p in enumerate(z_peers):
         crossing.append(send(x_own, own, z_s.at[d], z_r.at[d], (p, i)))
-    for e, p in enumerate(item_peers):
-        across[0, e] = send(x_own, own, xy_s.at[0, e], xy_r.at[0, e], (u, p))
-    pending.append(send(x_own, own, sib_s.at[0, items - 1], sib_r.at[0, items - 1], sibling))
+    for d in range(zs):
+        shard = 2 * lax.rem(z - d + zs, zs) + c
+        stages.append(exchange(
+            items, u, i, d, lambda q, n=shard: x_all.at[q, :, :, n], lambda q, h, n=shard: x_all.at[q, h, :, n],
+            sibling, xy_s, xy_r, sib_s, sib_r, sent, pending,
+        ))
+    stages[0][0](x_own)
     keep = pltpu.make_async_copy(x_own, own, local.at[0])
     keep.start()
     for d in range(1, zs):
         crossing[d - 1].wait_recv()
-        block = x_all.at[i, :, :, 2 * lax.rem(z - d + zs, zs) + c]
-        for e, p in enumerate(item_peers):
-            across[d, e] = send(block, block, xy_s.at[d, e], xy_r.at[d, e], (u, p))
-        pending.append(send(block, block, sib_s.at[d, items - 1], sib_r.at[d, items - 1], sibling))
-    for d in range(zs):
-        shard = 2 * lax.rem(z - d + zs, zs) + c
-        for e in range(items - 1):
-            across[d, e].wait_recv()
-            block = x_all.at[lax.rem(i - e - 1 + items, items), :, :, shard]
-            pending.append(send(block, block, sib_s.at[d, e], sib_r.at[d, e], sibling))
-    for copy in crossing + list(across.values()):
+        stages[d][0](x_all.at[i, :, :, 2 * lax.rem(z - d + zs, zs) + c])
+    for number in (1, 2):
+        for stage in stages:
+            stage[number]()
+    for copy in crossing + sent:
         copy.wait_send()
     for copy in pending:
         copy.wait()
@@ -372,7 +417,7 @@
             dma((zs := users // 2,)), dma((zs,)),
         ] + [dma((zs, items))] * 4 + [dma((items,)), dma((items,)), dma((2,))],
         compiler_params=pltpu.CompilerParams(
-            collective_id=1, has_side_effects=True, vmem_limit_bytes=48 * 2**20
+            collective_id=1, has_side_effects=True, vmem_limit_bytes=60 * 2**20
         ),
         name="solve_and_gather",
     )(table, start, *weights)
@@ -390,8 +435,8 @@
 
     conf = tile_conf.reshape(-1, width, width)
     held = held_conf.reshape(-1, width, width)
-    lists = (tile_item[0, 0], tile_user[0, 0], tile_count.reshape(-1, 1))
-    held_lists = (held_user[0, 0], held_item[0, 0], held_count.reshape(-1, 1))
+    lists = (tile_item[0, 0].T, tile_user[0, 0].T, tile_count[0])
+    held_lists = (held_user[0, 0].T, held_item[0, 0].T, held_count[0])
     table, tiles, held_tiles, user_lists, item_lists = spread(
         users, items, user_factors, conf, held, lists, held_lists
     )

time: 89.7 us -> 84.2 us (0.939)
  local copies, waits for them, and re-layouts: 12.9 us -> 4.18 us
  Pallas kernels: 75.7 us -> 79.1 us
    unnamed x16 -> x4, local copies, waits for them, and re-layouts: 8.3 us -> 3.55 us
    squeeze x4 -> x0, local copies, waits for them, and re-layouts: 3.09 us -> none  [the longest x2 1.56 us: shards(): lists = (tile_item[0, 0], tile_user[0, 0], tile_count.reshape(-1, 1))]
    pallas_call x1, Pallas kernels: 3.5 us -> 5.37 us  [place_tiles(): pl.pallas_call(functools.partial(place_kernel, item_blocks, user_blocks),...]
    reshape x2 -> x0, local copies, waits for them, and re-layouts: 1.47 us -> none  [the longest x1 0.74 us: shards(): held_lists = (held_user[0, 0], held_item[0, 0], held_count.reshape(-1, 1))]
    pallas_call x1, Pallas kernels: 31 us -> 32.2 us  [spread(): pl.pallas_call(functools.partial(spread_kernel, users, items), out_shape=...]
where the time goes in v3:
time: 84.2 us; the launch traced here: 83.9 us
  Pallas kernels  79.1 us (94%)
  local copies, waits for them, and re-layouts  4.18 us (5%)
    pallas_call x1, Pallas kernels, solve(): pl.pallas_call(functools.partial(solve_kernel, users, items), out_shape=[...  41.5 us
    pallas_call x1, Pallas kernels, spread(): pl.pallas_call(functools.partial(spread_kernel, users, items), out_shape=...  32.2 us
    pallas_call x1, Pallas kernels, place_tiles(): pl.pallas_call(functools.partial(place_kernel, item_blocks, user_blocks),...  5.37 us
    unnamed x4, local copies, waits for them, and re-layouts  3.55 us

profile of v3, /device:TPU:0, one launch (start us, length us, event | category | flops | bytes accessed | tf_op | source)
XLA Modules:
  0.0 83.9 jit_solution(15584844921411605449)
XLA Ops:
  0.6 0.0 copy-start
  0.6 32.2 %spread_inputs.1 = (bf16[8,4,2,128,256]{4,3,2,1,0:T(8,128)(2,1)}, bf16[8,256,128]{2,1,0:T(8,128)(2,1)}, bf16[4,256,128]{2,1,0:T(8,128)(2,1)}, s32[8,8,128]{2,1,0:T(8,128)}, s32[4,8,128]{2,1,0:T(8,128)}) custom-call(f32[512,256]{1,0:T(8,128)} %y_hbm.1, bf16[16,128,128]{2,1,0:T(8,128)(2,1)} %bitcast.22, bf16[8,128,128]{2,1,0:T(8,128)(2,1)} %bitcast.25, ...), custom_call_target="tpu_custom_call" | custom-call | tf_op jit(solution)/shard_map/spread_inputs/pallas_call | solution.py:222
  32.8 5.4 %place_tiles.1 = (f32[32,64,128]{2,1,0:T(8,128)}, f32[32,64,128]{2,1,0:T(8,128)}, f32[16,64,128]{2,1,0:T(8,128)}, f32[16,64,128]{2,1,0:T(8,128)}) custom-call(s32[8,8,128]{2,1,0:T(8,128)} %get-tuple-element.14.mu_ref, s32[4,8,128]{2,1,0:T(8,128)} %get-tuple-element.15.mi_ref, bf16[8,256,128]{2,1,0:T(8,128)(2,1)} %get-tuple-element.16.c_ref, ...), custom_call_target="tpu_custom_call" | custom-call | tf_op jit(solution)/shard_map/place_tiles/pallas_call | solution.py:286
  38.2 0.0 copy-done
  38.2 0.6 constant_dynamic-slice_fusion
  38.8 41.5 %solve_and_gather.1 = (f32[512,256]{1,0:T(8,128)}, f32[2,4,32,256]{3,2,1,0:T(8,128)}) custom-call(bf16[8,4,2,128,256]{4,3,2,1,0:T(8,128)(2,1)} %get-tuple-element.13.y_ref, f32[64,256]{1,0:T(8,128)} %bitcast.23, f32[32,64,128]{2,1,0:T(8,128)} %get-tuple-element.18.w_ref, f32[32,64,128]{2,1,0:T(8,128)} %get-tuple-element.19.right_ref, ...), custom_call_target="tpu_custom_call" | custom-call | tf_op jit(solution)/shard_map/solve_and_gather/pallas_call | solution.py:405
  80.4 1.9 %copy.16 = f32[512,256]{1,0:T(8,128)} copy(f32[512,256]{1,0:T(8,128)} %get-tuple-element.26) | data formatting | bytes 1048576
  82.2 1.7 %copy.17 = f32[256,256]{1,0:T(8,128)} copy(f32[256,256]{1,0:T(8,128)} %bitcast.24) | data formatting | bytes 524288
Async XLA Ops:
  0.6 37.6 %copy-start = (f32[512,256]{1,0:T(8,128)S(1)}, f32[512,256]{1,0:T(8,128)}, u32[]{:S(2)}) copy-start(f32[512,256]{1,0:T(8,128)} %param.11) | copy-start | bytes 1572868

commit v4 on v3

v4 whole, which is shorter than its diff:
```python
import functools

import jax
import jax.numpy as jnp
from jax import lax
from jax.experimental import pallas as pl
from jax.experimental.pallas import tpu as pltpu
from jax.sharding import PartitionSpec as P

ITERS = 2
RIDGE = 1.0
EPS = 1e-6
MESH = pl.DeviceIdType.MESH
ANY = pl.BlockSpec(memory_space=pl.ANY)
VMEM = pl.BlockSpec(memory_space=pltpu.VMEM)
HBM = pl.BlockSpec(memory_space=pltpu.HBM)
SMEM = pl.BlockSpec(memory_space=pltpu.SMEM)


def place(users, items):
    u = lax.axis_index("user")
    return lax.axis_index("item"), u, u // 2, lax.rem(u, 2)


def greet(devices):
    for device in devices:
        pl.semaphore_signal(pltpu.get_barrier_semaphore(), inc=1, device_id=device, device_id_type=MESH)


def await_greetings(devices):
    pl.semaphore_wait(pltpu.get_barrier_semaphore(), len(devices))


def send(src, dst, send_sem, recv_sem, device):
    copy = pltpu.make_async_remote_copy(
        src_ref=src, dst_ref=dst, send_sem=send_sem, recv_sem=recv_sem, device_id=device, device_id_type=MESH
    )
    copy.start()
    return copy


def pack_rows(tile_of, out, slots, peers):
    rows = out.shape[1] // slots
    group = max(1, 16 // rows)
    for first in range(0, slots, group):
        tiles = [tile_of(first + k) for k in range(group)]
        for p in range(peers):
            part = [t[p * rows:(p + 1) * rows] for t in tiles]
            part = part[0] if group == 1 else jnp.concatenate(part, axis=0)
            out[p, first * rows:(first + group) * rows, :] = part.astype(out.dtype)


def halves(value):
    high = value.astype(jnp.bfloat16)
    return high, (value - high.astype(jnp.float32)).astype(jnp.bfloat16)


def dot(a, b, contract):
    return lax.dot_general(a, b, (((1,), (contract,)), ((), ())), preferred_element_type=jnp.float32)


def product(value, high, low, contract):
    n = value.shape[0]
    top, bottom = halves(value)
    both = dot(jnp.concatenate([top, bottom], axis=0), high, contract)
    return both[:n] + both[n:] + dot(top, low, contract)


def describe(out, joined, named, counts, per_owner):
    cap, owners = joined.shape
    for owner in range(owners):
        for k in range(cap):
            code = jnp.where(k < counts[0, owner], joined[k, owner] * per_owner + named[k, owner], -1)
            s = owner * cap + k
            out[s:s + 1, :] = jnp.full((1, out.shape[1]), code, jnp.int32)


def place_tiles(codes, tiles, weight, right, per_owner):
    blocks, rows, width = weight.shape
    sources, slots = tiles.shape[0], codes.shape[1]
    part = tiles.shape[1] // slots
    cap = slots * per_owner // blocks
    spans = rows // part

    def step(b, carry):
        owner, inner = b // per_owner, lax.rem(b, per_owner)
        sums = [jnp.zeros((part, width), jnp.float32) for _ in range(spans)]
        counts = [jnp.zeros((8, width), jnp.float32) for _ in range(spans)]
        for source in range(sources):
            first = pl.multiple_of(owner * (cap * part), cap * part)
            both = tiles[source, pl.ds(first, cap * part), :].astype(jnp.float32)
            for k in range(cap):
                tile = both[k * part:(k + 1) * part]
                code = codes[source, pl.ds(owner * cap + k, 1), :]
                for n in range(spans):
                    hit = jnp.broadcast_to(code == n * per_owner + inner, (8, width))
                    counts[n] = counts[n] + jnp.where(hit, 1.0, 0.0)
                    whole = jnp.broadcast_to(code == n * per_owner + inner, (part, width))
                    sums[n] = sums[n] + jnp.where(whole, tile, 0.0)
        for n in range(spans):
            weight[b, n * part:(n + 1) * part, :] = sums[n] + 1.0
            right[b, n * part:(n + 1) * part, :] = sums[n] + jnp.concatenate([counts[n]] * (part // 8), axis=0)
        return carry

    lax.fori_loop(0, blocks, step, 0)


def exchange(items, u, i, d, block, half, sibling, xy_s, xy_r, sib_s, sib_r, sent, pending):
    direct, relays = [], []

    def mirror(q, slot):
        pending.append(send(block(q), block(q), sib_s.at[d, slot], sib_r.at[d, slot], sibling))

    def hop(src, slot, p):
        copy = send(src, src, xy_s.at[d, slot], xy_r.at[d, slot], (u, p))
        sent.append(copy)
        return copy

    if items != 4:
        def first(src):
            for e in range(1, items):
                copy = send(src, block(i), xy_s.at[d, e], xy_r.at[d, e], (u, lax.rem(i + e, items)))
                direct.append(copy)
                sent.append(copy)
            pending.append(send(src, block(i), sib_s.at[d, 0], sib_r.at[d, 0], sibling))

        def second():
            return None

        def third():
            for e in range(1, items):
                direct[e - 1].wait_recv()
                mirror(lax.rem(i - e + items, items), e)

        return first, second, third

    flip = 1 - 2 * lax.rem(i, 2)
    beside, behind = i + flip, lax.rem(i + 2, 4)
    opposite = behind + flip

    def first(src):
        for slot, p in enumerate((beside, behind)):
            copy = send(src, block(i), xy_s.at[d, slot], xy_r.at[d, slot], (u, p))
            direct.append(copy)
            sent.append(copy)
        pending.append(send(src, block(i), sib_s.at[d, 3], sib_r.at[d, 3], sibling))

    def second():
        direct[0].wait_recv()
        relays.append(hop(half(beside, 0), 3, behind))
        mirror(beside, 0)
        direct[1].wait_recv()
        relays.append(hop(half(behind, 1), 2, beside))
        mirror(behind, 1)

    def third():
        for copy in relays:
            copy.wait_recv()
        mirror(opposite, 2)

    return first, second, third


def conjugate(chunk_of, weight, right, x, rows, rank, chunks):
    per_chunk = weight.shape[0] // chunks

    def wide(ref, n):
        return jnp.concatenate([ref[n * per_chunk + k] for k in range(per_chunk)], axis=1)

    def sweep(coefficients):
        def step(n, total):
            top, bottom = chunk_of(n)
            return total + product(coefficients(n, top, bottom), top, bottom, 0)

        return lax.fori_loop(0, chunks, step, jnp.zeros((rows, rank), jnp.float32), unroll=2)

    def operator(vector):
        return sweep(lambda n, top, bottom: product(vector, top, bottom, 1) * wide(weight, n)) + RIDGE * vector

    if x is None:
        x = jnp.zeros((rows, rank), jnp.float32)
        residual = sweep(lambda n, top, bottom: wide(right, n))
    else:
        residual = sweep(
            lambda n, top, bottom: wide(right, n) - product(x, top, bottom, 1) * wide(weight, n)
        ) - RIDGE * x
    direction = residual
    norm = jnp.sum(residual * residual, axis=1, keepdims=True)
    for iteration in range(ITERS):
        image = operator(direction)
        alpha = norm / (jnp.sum(direction * image, axis=1, keepdims=True) + EPS)
        x = x + alpha * direction
        if iteration + 1 < ITERS:
            residual = residual - alpha * image
            following = jnp.sum(residual * residual, axis=1, keepdims=True)
            direction = residual + following / (norm + EPS) * direction
            norm = following
    return x


def merge_rows(value):
    if value.shape[-2] % 16:
        return value.astype(jnp.float32).reshape(-1, value.shape[-1]).astype(value.dtype)
    return value.reshape(-1, value.shape[-1])


def sweep_kernel(users, items, y_hbm, conf_hbm, held_hbm, start_hbm, ti_ref, tu_ref, tc_ref, hu_ref, hi_ref, hc_ref,
                 new_ref, fold_ref,
                 y_out, c_out, h_out, mu_out, mi_out, y_ref, conf_ref, held_ref, start_ref,
                 y_send, c_send, h_send, mu_send, mi_send, w_ref, right_ref, v_ref, held_right_ref, x_all, x_own, f_own,
                 z_s, z_r, xy_s, xy_r, sib_s, sib_r, own_s, own_r, c_s, c_r, h_s, h_r, mu_s, mu_r, mi_s, mi_r,
                 xz_s, xz_r, xxy_s, xxy_r, xsib_s, xsib_r, f_s, f_r, local):
    zs = users // 2
    i, u, z, c = place(users, items)
    sibling = (2 * z + 1 - c, i)
    quarter = y_send.shape[2]
    user_peers = [lax.rem(u + k, users) for k in range(1, users)]
    item_peers = [lax.rem(i + e, items) for e in range(1, items)]
    neighbours = [(p, i) for p in user_peers] + [(u, p) for p in item_peers]
    loads = [
        pltpu.make_async_copy(y_hbm, y_ref, local.at[5]),
        pltpu.make_async_copy(held_hbm, held_ref, local.at[6]),
        pltpu.make_async_copy(conf_hbm, conf_ref, local.at[7]),
        pltpu.make_async_copy(start_hbm.at[:, u], start_ref, local.at[8]),
    ]
    for load in loads:
        load.start()
    greet(neighbours)
    describe(mu_send, ti_ref, tu_ref, tc_ref, w_ref.shape[0] // users)
    describe(mi_send, hu_ref, hi_ref, hc_ref, v_ref.shape[0] // items)
    loads[0].wait()
    for q in range(items):
        top, bottom = halves(y_ref[q * quarter:(q + 1) * quarter, :])
        y_send[q, 0] = top
        y_send[q, 1] = bottom
    await_greetings(neighbours)

    pending, tiled = [], []
    crossing = []
    for d in range(1, zs):
        peer = 2 * lax.rem(z + d, zs) + c
        crossing.append(send(y_send.at[i], y_out.at[u, i], z_s.at[d], z_r.at[d], (peer, i)))
    pending.append(send(y_send, y_out.at[u], own_s, own_r, sibling))
    keep = [pltpu.make_async_copy(y_send, y_out.at[u], local.at[0])]
    keep[0].start()

    held_slots = held_ref.shape[0]
    loads[1].wait()
    pack_rows(lambda s: held_ref[s].astype(jnp.float32), h_send, held_slots, items)
    for e, p in enumerate(item_peers):
        tiled.append(send(h_send.at[p], h_out.at[i], h_s.at[e], h_r.at[e], (u, p)))
        tiled.append(send(mi_send, mi_out.at[i], mi_s.at[e], mi_r.at[e], (u, p)))
    for k, p in enumerate(user_peers):
        tiled.append(send(mu_send, mu_out.at[u], mu_s.at[k], mu_r.at[k], (p, i)))
    slots = conf_ref.shape[0]
    loads[2].wait()
    pack_rows(lambda s: conf_ref[s].astype(jnp.float32).T, c_send, slots, users)
    for k, p in enumerate(user_peers):
        tiled.append(send(c_send.at[p], c_out.at[u], c_s.at[k], c_r.at[k], (p, i)))
    keep.append(pltpu.make_async_copy(c_send.at[u], c_out.at[u], local.at[1]))
    keep.append(pltpu.make_async_copy(h_send.at[i], h_out.at[i], local.at[2]))
    keep.append(pltpu.make_async_copy(mu_send, mu_out.at[u], local.at[3]))
    keep.append(pltpu.make_async_copy(mi_send, mi_out.at[i], local.at[4]))
    for copy in keep[1:]:
        copy.start()

    sent, stages = [], []
    for d in range(1, zs):
        shard = 2 * lax.rem(z - d + zs, zs) + c
        stages.append(exchange(
            items, u, i, d, lambda q, n=shard: y_out.at[n, q], lambda q, h, n=shard: y_out.at[n, q, h],
            sibling, xy_s, xy_r, sib_s, sib_r, sent, pending,
        ))
    for d in range(1, zs):
        crossing[d - 1].wait_recv()
        stages[d - 1][0](y_out.at[2 * lax.rem(z - d + zs, zs) + c, i])
    for stage in stages:
        stage[1]()
    for copy in tiled:
        copy.wait()
    for copy in keep:
        copy.wait()
    loads[3].wait()
    place_tiles(mu_out, c_out, w_ref, right_ref, w_ref.shape[0] // users)
    place_tiles(mi_out, h_out, v_ref, held_right_ref, v_ref.shape[0] // items)
    for stage in stages:
        stage[2]()
    for copy in crossing + sent:
        copy.wait_send()
    for copy in pending:
        copy.wait()

    _, blocks, part, rank = x_own.shape
    x = conjugate(
        lambda n: (merge_rows(y_out[n, :, 0]), merge_rows(y_out[n, :, 1])),
        w_ref, right_ref, start_ref[...].reshape(blocks * part, rank), blocks * part, rank, users,
    )
    top, bottom = halves(x)
    x_own[0] = top.astype(jnp.float32).reshape(blocks, part, rank).astype(jnp.bfloat16)
    x_own[1] = bottom.astype(jnp.float32).reshape(blocks, part, rank).astype(jnp.bfloat16)
    z_peers = [2 * lax.rem(z + d, zs) + c for d in range(1, zs)]
    crossing, sent, pending, stages = [], [], [], []
    own = x_all.at[i, :, :, u]
    for d, p in enumerate(z_peers):
        crossing.append(send(x_own, own, xz_s.at[d], xz_r.at[d], (p, i)))
    for d in range(zs):
        shard = 2 * lax.rem(z - d + zs, zs) + c
        stages.append(exchange(
            items, u, i, d, lambda q, n=shard: x_all.at[q, :, :, n], lambda q, h, n=shard: x_all.at[q, h, :, n],
            sibling, xxy_s, xxy_r, xsib_s, xsib_r, sent, pending,
        ))
    stages[0][0](x_own)
    keep = pltpu.make_async_copy(x_own, own, local.at[9])
    keep.start()
    for d in range(1, zs):
        crossing[d - 1].wait_recv()
        stages[d][0](x_all.at[i, :, :, 2 * lax.rem(z - d + zs, zs) + c])
    for number in (1, 2):
        for stage in stages:
            stage[number]()
    for copy in crossing + sent:
        copy.wait_send()
    for copy in pending:
        copy.wait()
    keep.wait()

    new_ref[...] = merge_rows(x_all[i, 0]).astype(jnp.float32) + merge_rows(x_all[i, 1]).astype(jnp.float32)
    held_blocks, held_part, _ = f_own.shape
    folded = conjugate(
        lambda n: (merge_rows(x_all[n, 0]), merge_rows(x_all[n, 1])),
        v_ref, held_right_ref, None, held_blocks * held_part, rank, items,
    )
    f_own[...] = folded.reshape(held_blocks, held_part, rank)
    mine = fold_ref.at[:, i]
    copies = [send(f_own, mine, f_s.at[e], f_r.at[e], (u, p)) for e, p in enumerate(item_peers)]
    last = pltpu.make_async_copy(f_own, mine, local.at[10])
    last.start()
    for copy in copies:
        copy.wait()
    last.wait()


def sweep(users, items, factors, conf, held, start, lists, held_lists):
    rows, rank = factors.shape
    slots, width = conf.shape[0], conf.shape[1]
    held_slots = held.shape[0]
    item_blocks, _, part, _ = start.shape
    user_blocks, held_blocks, held_part = rows // width, 2, width // items
    zs = users // 2
    y_piece = (2, rows // items, rank)
    c_piece, h_piece = (slots * part, width), (held_slots * held_part, width)
    bf16, f32, i32 = jnp.bfloat16, jnp.float32, jnp.int32
    item_side = (users * user_blocks, item_blocks * part, width)
    held_side = (items * item_blocks, held_blocks * held_part, width)
    dma = pltpu.SemaphoreType.DMA
    rounds = [dma((zs,)), dma((zs,))] + [dma((zs, items))] * 4
    return pl.pallas_call(
        functools.partial(sweep_kernel, users, items),
        out_shape=[
            jax.ShapeDtypeStruct((item_blocks * width, rank), f32),
            jax.ShapeDtypeStruct((held_blocks, items, held_part, rank), f32),
        ],
        in_specs=[HBM] * 4 + [SMEM] * 6,
        out_specs=[VMEM, VMEM],
        scratch_shapes=[
            pltpu.VMEM((users, items) + y_piece, bf16),
            pltpu.VMEM((users,) + c_piece, bf16),
            pltpu.VMEM((items,) + h_piece, bf16),
            pltpu.VMEM((users, slots, width), i32),
            pltpu.VMEM((items, held_slots, width), i32),
            pltpu.VMEM((rows, rank), f32),
            pltpu.VMEM(conf.shape, bf16),
            pltpu.VMEM(held.shape, bf16),
            pltpu.VMEM((item_blocks, part, rank), f32),
            pltpu.VMEM((items,) + y_piece, bf16),
            pltpu.VMEM((users,) + c_piece, bf16),
            pltpu.VMEM((items,) + h_piece, bf16),
            pltpu.VMEM((slots, width), i32),
            pltpu.VMEM((held_slots, width), i32),
            pltpu.VMEM(item_side, f32),
            pltpu.VMEM(item_side, f32),
            pltpu.VMEM(held_side, f32),
            pltpu.VMEM(held_side, f32),
            pltpu.VMEM((items, 2, item_blocks, users, part, rank), bf16),
            pltpu.VMEM((2, item_blocks, part, rank), bf16),
            pltpu.VMEM((held_blocks, held_part, rank), f32),
        ] + rounds + [dma, dma, dma((users,)), dma((users,)), dma((items,)), dma((items,)),
                      dma((users,)), dma((users,)), dma((items,)), dma((items,))]
        + rounds + [dma((items,)), dma((items,)), dma((11,))],
        compiler_params=pltpu.CompilerParams(
            collective_id=0, has_side_effects=True, vmem_limit_bytes=60 * 2**20
        ),
        name="sweep",
    )(factors, conf, held, start, *lists, *held_lists)


def shards(user_factors, item_factors, tile_user, tile_item, tile_count, tile_conf,
           held_user, held_item, held_count, held_conf):
    users, items = lax.axis_size("user"), lax.axis_size("item")
    width = tile_conf.shape[-1]
    rank = user_factors.shape[1]
    new_items, folded = sweep(
        users, items, user_factors,
        tile_conf.reshape(-1, width, width), held_conf.reshape(-1, width, width),
        item_factors.reshape(item_factors.shape[0] // width, users, width // users, rank),
        (tile_item[0, 0].T, tile_user[0, 0].T, tile_count[0]),
        (held_user[0, 0].T, held_item[0, 0].T, held_count[0]),
    )
    return new_items, folded.reshape(-1, rank)


def solution(mesh):
    in_specs = (
        P("user", None),
        P("item", None),
        P("item", "user", None, None),
        P("item", "user", None, None),
        P("item", "user", None),
        P("item", "user", None, None, None, None),
        P("user", "item", None, None),
        P("user", "item", None, None),
        P("user", "item", None),
        P("user", "item", None, None, None, None),
    )
    out_specs = (P("item", None), P("user", None))
    return jax.shard_map(shards, mesh=mesh, in_specs=in_specs, out_specs=out_specs, check_vma=False)
```

time: 84.2 us -> 77.4 us (0.919)
  Pallas kernels: 79.1 us -> 74 us
  local copies, waits for them, and re-layouts: 4.18 us -> 2.62 us
    pallas_call x3 -> x1, Pallas kernels: 79.1 us -> 74 us  [sweep(): pl.pallas_call(functools.partial(sweep_kernel, users, items), out_shape=[...]
    unnamed x4, local copies, waits for them, and re-layouts: 3.55 us -> 2.62 us
where the time goes in v4:
time: 77.4 us; the launch traced here: 77.3 us
  Pallas kernels  74 us (96%)
  local copies, waits for them, and re-layouts  2.62 us (3%)
    pallas_call x1, Pallas kernels, sweep(): pl.pallas_call(functools.partial(sweep_kernel, users, items), out_shape=[...  74 us
    unnamed x4, local copies, waits for them, and re-layouts  2.62 us

profile of v4, /device:TPU:0, one launch (start us, length us, event | category | flops | bytes accessed | tf_op | source)
XLA Modules:
  0.0 77.3 jit_solution(16814381495674549837)
XLA Ops:
  0.6 74.0 %sweep.1 = (f32[512,256]{1,0:T(8,128)}, f32[2,4,32,256]{3,2,1,0:T(8,128)}) custom-call(f32[512,256]{1,0:T(8,128)} %y_hbm.1, bf16[16,128,128]{2,1,0:T(8,128)(2,1)} %bitcast.18, bf16[8,128,128]{2,1,0:T(8,128)(2,1)} %bitcast.20, f32[4,8,16,256]{3,2,1,0:T(8,128)} %bitcast.19, s32[2,8]{1,0:T(2,128)} %bitcast.22, s32[2,8]{1,0:T(2,128)} %bitcast.23, ...), custom_call_target="tpu_custom_call" | custom-call | tf_op jit(solution)/shard_map/sweep/pallas_call | solution.py:357
  74.6 0.0 copy-start
  74.6 1.9 %copy.14 = f32[512,256]{1,0:T(8,128)} copy(f32[512,256]{1,0:T(8,128)} %get-tuple-element.8) | data formatting | bytes 1048576
  76.6 0.0 copy-done
  76.6 0.7 copy.15
Async XLA Ops:
  74.6 1.9 %copy-start = (f32[2,4,32,256]{3,2,1,0:T(8,128)S(1)}, f32[2,4,32,256]{3,2,1,0:T(8,128)}, u32[]{:S(2)}) copy-start(f32[2,4,32,256]{3,2,1,0:T(8,128)} %get-tuple-element.5) | copy-start | bytes 786436

commit v5 on v4

--- a/solution.py
+++ b/solution.py
@@ -103,6 +103,46 @@
         return carry
 
     lax.fori_loop(0, blocks, step, 0)
+
+
+def by_distance(z, zs):
+    near = jnp.minimum(z, zs - 1 - z)
+    order = []
+    for k in range(zs - 1):
+        beside = z - (k // 2 + 1) if k % 2 == 0 else z + (k // 2 + 1)
+        step = k - near + 1
+        beyond = jnp.where(2 * z < zs - 1, z + step, z - step)
+        order.append(jnp.where(k < 2 * near, beside, beyond))
+    return order
+
+
+def chain(i, z, c, zs, order, own, block, z_s, z_r):
+    def to(src, dst, slot, n, place):
+        inside = jnp.logical_and(place >= 0, place < zs)
+        device = (2 * jnp.clip(place, 0, zs - 1) + c, i)
+        return inside, pltpu.make_async_remote_copy(
+            src_ref=src, dst_ref=dst, send_sem=z_s.at[slot], recv_sem=z_r.at[n],
+            device_id=device, device_id_type=MESH,
+        )
+
+    moves = [to(own, block(z), 0, z, z + 1), to(own, block(z), 1, z, z - 1)]
+    onward = [to(block(n), block(n), 2 + k, n, jnp.where(n < z, z + 1, z - 1)) for k, n in enumerate(order)]
+
+    def start(move):
+        pl.when(move[0])(lambda: move[1].start())
+
+    for move in moves:
+        start(move)
+
+    def take(k):
+        onward[k][1].wait_recv()
+        start(onward[k])
+
+    def close():
+        for inside, copy in moves + onward:
+            pl.when(inside)(copy.wait_send)
+
+    return take, close
 
 
 def exchange(items, u, i, d, block, half, sibling, xy_s, xy_r, sib_s, sib_r, sent, pending):
@@ -236,10 +276,8 @@
     await_greetings(neighbours)
 
     pending, tiled = [], []
-    crossing = []
-    for d in range(1, zs):
-        peer = 2 * lax.rem(z + d, zs) + c
-        crossing.append(send(y_send.at[i], y_out.at[u, i], z_s.at[d], z_r.at[d], (peer, i)))
+    order = by_distance(z, zs)
+    take, close = chain(i, z, c, zs, order, y_send.at[i], lambda n: y_out.at[2 * n + c, i], z_s, z_r)
     pending.append(send(y_send, y_out.at[u], own_s, own_r, sibling))
     keep = [pltpu.make_async_copy(y_send, y_out.at[u], local.at[0])]
     keep[0].start()
@@ -265,15 +303,15 @@
         copy.start()
 
     sent, stages = [], []
-    for d in range(1, zs):
-        shard = 2 * lax.rem(z - d + zs, zs) + c
+    for d, n in enumerate(order):
+        shard = 2 * n + c
         stages.append(exchange(
             items, u, i, d, lambda q, n=shard: y_out.at[n, q], lambda q, h, n=shard: y_out.at[n, q, h],
             sibling, xy_s, xy_r, sib_s, sib_r, sent, pending,
         ))
-    for d in range(1, zs):
-        crossing[d - 1].wait_recv()
-        stages[d - 1][0](y_out.at[2 * lax.rem(z - d + zs, zs) + c, i])
+    for d, n in enumerate(order):
+        take(d)
+        stages[d][0](y_out.at[2 * n + c, i])
     for stage in stages:
         stage[1]()
     for copy in tiled:
@@ -285,7 +323,8 @@
     place_tiles(mi_out, h_out, v_ref, held_right_ref, v_ref.shape[0] // items)
     for stage in stages:
         stage[2]()
-    for copy in crossing + sent:
+    close()
+    for copy in sent:
         copy.wait_send()
     for copy in pending:
         copy.wait()
@@ -298,13 +337,11 @@
     top, bottom = halves(x)
     x_own[0] = top.astype(jnp.float32).reshape(blocks, part, rank).astype(jnp.bfloat16)
     x_own[1] = bottom.astype(jnp.float32).reshape(blocks, part, rank).astype(jnp.bfloat16)
-    z_peers = [2 * lax.rem(z + d, zs) + c for d in range(1, zs)]
-    crossing, sent, pending, stages = [], [], [], []
+    sent, pending, stages = [], [], []
     own = x_all.at[i, :, :, u]
-    for d, p in enumerate(z_peers):
-        crossing.append(send(x_own, own, xz_s.at[d], xz_r.at[d], (p, i)))
-    for d in range(zs):
-        shard = 2 * lax.rem(z - d + zs, zs) + c
+    take, close = chain(i, z, c, zs, order, x_own, lambda n: x_all.at[i, :, :, 2 * n + c], xz_s, xz_r)
+    for d, n in enumerate([z] + order):
+        shard = 2 * n + c
         stages.append(exchange(
             items, u, i, d, lambda q, n=shard: x_all.at[q, :, :, n], lambda q, h, n=shard: x_all.at[q, h, :, n],
             sibling, xxy_s, xxy_r, xsib_s, xsib_r, sent, pending,
@@ -312,13 +349,14 @@
     stages[0][0](x_own)
     keep = pltpu.make_async_copy(x_own, own, local.at[9])
     keep.start()
-    for d in range(1, zs):
-        crossing[d - 1].wait_recv()
-        stages[d][0](x_all.at[i, :, :, 2 * lax.rem(z - d + zs, zs) + c])
+    for d, n in enumerate(order):
+        take(d)
+        stages[d + 1][0](x_all.at[i, :, :, 2 * n + c])
     for number in (1, 2):
         for stage in stages:
             stage[number]()
-    for copy in crossing + sent:
+    close()
+    for copy in sent:
         copy.wait_send()
     for copy in pending:
         copy.wait()
@@ -353,7 +391,7 @@
     item_side = (users * user_blocks, item_blocks * part, width)
     held_side = (items * item_blocks, held_blocks * held_part, width)
     dma = pltpu.SemaphoreType.DMA
-    rounds = [dma((zs,)), dma((zs,))] + [dma((zs, items))] * 4
+    rounds = [dma((zs + 1,)), dma((zs,))] + [dma((zs, items))] * 4
     return pl.pallas_call(
         functools.partial(sweep_kernel, users, items),
         out_shape=[

time: 77.4 us -> 84.1 us (1.087)
  Pallas kernels: 74 us -> 80.7 us
    pallas_call x1, Pallas kernels: 74 us -> 80.7 us  [sweep(): pl.pallas_call(functools.partial(sweep_kernel, users, items), out_shape=[...]
where the time goes in v5:
time: 84.1 us; the launch traced here: 83.9 us
  Pallas kernels  80.7 us (96%)
  local copies, waits for them, and re-layouts  2.62 us (3%)
    pallas_call x1, Pallas kernels, sweep(): pl.pallas_call(functools.partial(sweep_kernel, users, items), out_shape=[...  80.7 us
    unnamed x4, local copies, waits for them, and re-layouts  2.62 us

profile of v5, /device:TPU:0, one launch (start us, length us, event | category | flops | bytes accessed | tf_op | source)
XLA Modules:
  0.0 83.9 jit_solution(10190613570692955359)
XLA Ops:
  0.6 80.7 %sweep.1 = (f32[512,256]{1,0:T(8,128)}, f32[2,4,32,256]{3,2,1,0:T(8,128)}) custom-call(f32[512,256]{1,0:T(8,128)} %y_hbm.1, bf16[16,128,128]{2,1,0:T(8,128)(2,1)} %bitcast.18, bf16[8,128,128]{2,1,0:T(8,128)(2,1)} %bitcast.20, f32[4,8,16,256]{3,2,1,0:T(8,128)} %bitcast.19, s32[2,8]{1,0:T(2,128)} %bitcast.22, s32[2,8]{1,0:T(2,128)} %bitcast.23, ...), custom_call_target="tpu_custom_call" | custom-call | tf_op jit(solution)/shard_map/sweep/pallas_call | solution.py:395
  81.3 0.0 copy-start
  81.3 1.9 %copy.14 = f32[512,256]{1,0:T(8,128)} copy(f32[512,256]{1,0:T(8,128)} %get-tuple-element.8) | data formatting | bytes 1048576
  83.2 0.0 copy-done
  83.2 0.7 copy.15
Async XLA Ops:
  81.3 1.9 %copy-start = (f32[2,4,32,256]{3,2,1,0:T(8,128)S(1)}, f32[2,4,32,256]{3,2,1,0:T(8,128)}, u32[]{:S(2)}) copy-start(f32[2,4,32,256]{3,2,1,0:T(8,128)} %get-tuple-element.5) | copy-start | bytes 786436

commit v6 on v4

--- a/solution.py
+++ b/solution.py
@@ -172,7 +172,7 @@
             top, bottom = chunk_of(n)
             return total + product(coefficients(n, top, bottom), top, bottom, 0)
 
-        return lax.fori_loop(0, chunks, step, jnp.zeros((rows, rank), jnp.float32), unroll=2)
+        return lax.fori_loop(0, chunks, step, jnp.zeros((rows, rank), jnp.float32), unroll=4)
 
     def operator(vector):
         return sweep(lambda n, top, bottom: product(vector, top, bottom, 1) * wide(weight, n)) + RIDGE * vector

time: 77.4 us -> 75.5 us (0.975)
  Pallas kernels: 74 us -> 72.1 us
    pallas_call x1, Pallas kernels: 74 us -> 72.1 us  [sweep(): pl.pallas_call(functools.partial(sweep_kernel, users, items), out_shape=[...]
where the time goes in v6:
time: 75.5 us; the launch traced here: 75.4 us
  Pallas kernels  72.1 us (95%)
  local copies, waits for them, and re-layouts  2.62 us (3%)
    pallas_call x1, Pallas kernels, sweep(): pl.pallas_call(functools.partial(sweep_kernel, users, items), out_shape=[...  72.1 us
    unnamed x4, local copies, waits for them, and re-layouts  2.62 us

profile of v6, /device:TPU:0, one launch (start us, length us, event | category | flops | bytes accessed | tf_op | source)
XLA Modules:
  0.0 75.4 jit_solution(6764330921050365688)
XLA Ops:
  0.6 72.1 %sweep.1 = (f32[512,256]{1,0:T(8,128)}, f32[2,4,32,256]{3,2,1,0:T(8,128)}) custom-call(f32[512,256]{1,0:T(8,128)} %y_hbm.1, bf16[16,128,128]{2,1,0:T(8,128)(2,1)} %bitcast.18, bf16[8,128,128]{2,1,0:T(8,128)(2,1)} %bitcast.20, f32[4,8,16,256]{3,2,1,0:T(8,128)} %bitcast.19, s32[2,8]{1,0:T(2,128)} %bitcast.22, s32[2,8]{1,0:T(2,128)} %bitcast.23, ...), custom_call_target="tpu_custom_call" | custom-call | tf_op jit(solution)/shard_map/sweep/pallas_call | solution.py:357
  72.7 0.0 copy-start
  72.8 1.9 %copy.14 = f32[512,256]{1,0:T(8,128)} copy(f32[512,256]{1,0:T(8,128)} %get-tuple-element.8) | data formatting | bytes 1048576
  74.7 0.0 copy-done
  74.7 0.7 copy.15
Async XLA Ops:
  72.7 1.9 %copy-start = (f32[2,4,32,256]{3,2,1,0:T(8,128)S(1)}, f32[2,4,32,256]{3,2,1,0:T(8,128)}, u32[]{:S(2)}) copy-start(f32[2,4,32,256]{3,2,1,0:T(8,128)} %get-tuple-element.5) | copy-start | bytes 786436
